TPU v7x, 512 devices: a whole 4x8x8 slice. The times are simulated.
512 devices in a mesh: seq: 32 (over y, x), tensor: 16 (over z, core).
Axes of the slice: x: 4, y: 8, z: 8, core: 2. Of those that a mesh axis runs over, the one named last changes fastest.
Arguments:
- hidden: bfloat16 [2048, 28672], P('seq', 'tensor'), may hold values from -6 to 6
- down_weight: bfloat16 [28672, 8192], P('tensor', 'seq'), may hold values from -0.03125 to 0.03125
- delta_blocks: bfloat16 [32, 4096, 4096], P('seq', 'tensor'), may hold values from -0.08984375 to 0.08984375
- block_rows: int32 [32, 16, 256], replicated, may hold values from -1 to 27, as said below
- block_cols: int32 [32, 16, 256], replicated, may hold values from -1 to 127, as said below
- tenant_ids: int32 [2048], replicated, may hold values from 0 to 31, as said below
- tenant_lists: int32 [32, 128], replicated, may hold values from -1 to 2047, as said below
Outputs:
- mixed: bfloat16 [2048, 8192], P('tensor', 'seq')
Inputs may be any that keep to these rules, and one draw needn't show every extreme that they name: `tenant_ids`: every variant names at least one and at most 128 tokens, and some variant names exactly 128. `tenant_lists`: row k lists, in ascending order, exactly the tokens whose tenant_ids entry is k, then -1 in the remaining slots. `block_rows`: slots g * 8 to (g + 1) * 8 - 1 of a list hold blocks whose column lies in g * 4 to (g + 1) * 4 - 1; live slots of one group come first, name distinct blocks, and in each list some group is full. Empty slots hold -1 here and in block_cols. `block_cols`: -1 marks an empty slot, exactly where block_rows holds -1.
All inputs are finite; a program needn't handle non-finite values.
Results may differ from a plain program's by a relative error of at most 0.0075.
Values may be sent and summed in bfloat16 or wider, within the bound.
No kernel may reach another device: no remote copies, remote signals or barrier semaphores. Data moves between devices by JAX's collectives and lax.ppermute only.
A program may use at most 128 MiB of HBM per device.

v0:
```python
import jax
import jax.numpy as jnp
from jax import lax
from jax.sharding import PartitionSpec as P

BLK = 64


def per_device(hidden, down_weight, delta_blocks, block_rows, block_cols, tenant_ids, tenant_lists):
    seq_index = lax.axis_index("seq")
    tensor_index = lax.axis_index("tensor")
    seq_count = lax.axis_size("seq")
    variant_count, capacity = tenant_lists.shape
    ff_local, width_local = down_weight.shape
    slot_count = delta_blocks.shape[1]
    per_group = slot_count // seq_count
    col_blocks = width_local // BLK
    row_blocks = ff_local // BLK
    own_list = lax.dynamic_index_in_dim(tenant_lists, seq_index, 0, False)
    start_rows = jnp.zeros((capacity, ff_local), jnp.bfloat16)
    piece = lax.all_gather(hidden, "seq", axis=0, tiled=True)
    picked = start_rows
    count = piece.shape[0]
    inside = (own_list >= 0) & (own_list < count)
    taken = jnp.take(piece, jnp.clip(own_list, 0, count - 1), axis=0)
    product = jnp.dot(piece, down_weight, preferred_element_type=jnp.float32)
    base, picked = (product, jnp.where(inside[:, None], taken, picked))
    shard_rows = lax.dynamic_index_in_dim(
        lax.dynamic_index_in_dim(block_rows, seq_index, 0, False), tensor_index, 0, False
    )
    shard_cols = lax.dynamic_index_in_dim(
        lax.dynamic_index_in_dim(block_cols, seq_index, 0, False), tensor_index, 0, False
    )
    matrices = delta_blocks[0].reshape(slot_count, BLK, BLK)
    pieces = jnp.take(
        picked.reshape(capacity, row_blocks, BLK), jnp.clip(shard_rows, 0, row_blocks - 1), axis=1
    )
    products = jnp.einsum("tnb,nbc->tnc", pieces, matrices, preferred_element_type=jnp.float32)
    grouped = products.reshape(capacity, seq_count, per_group, BLK)
    offsets = (
        shard_cols.reshape(seq_count, per_group)
        - (jnp.arange(seq_count, dtype=jnp.int32) * col_blocks)[:, None]
    )
    selector = (offsets[:, :, None] == jnp.arange(col_blocks, dtype=jnp.int32)).astype(jnp.float32)
    placed = jnp.einsum("tgbx,gbc->tgcx", grouped, selector, precision=lax.Precision.HIGHEST)
    received = lax.all_to_all(
        placed.reshape(1, capacity, seq_count * width_local).astype(jnp.bfloat16),
        "seq",
        split_axis=2,
        concat_axis=0,
        tiled=True,
    ).astype(jnp.float32)
    flat = received.reshape(variant_count * capacity, width_local)
    match = tenant_ids[:, None] == jnp.arange(variant_count, dtype=jnp.int32)[None, :]
    running = jnp.cumsum(match.astype(jnp.int32), axis=0) - 1
    rank = jnp.sum(jnp.where(match, running, 0), axis=1)
    delta_rows = jnp.take(flat, tenant_ids * capacity + rank, axis=0)
    total = base + delta_rows
    return lax.psum_scatter(total, "tensor", scatter_dimension=0, tiled=True).astype(jnp.bfloat16)


def solution(mesh):
    return jax.shard_map(
        per_device,
        mesh=mesh,
        in_specs=(
            P("seq", "tensor"),
            P("tensor", "seq"),
            P("seq", "tensor", None),
            P(),
            P(),
            P(),
            P(),
        ),
        out_specs=P("tensor", "seq"),
        check_vma=False,
    )
```

profile of v0, /device:TPU:1, one launch (start us, length us, event | category | flops | bytes accessed | tf_op | source)
XLA Modules:
  0.0 371.8 jit_solution(5420155747965457671)
XLA Ops:
  6.5 0.0 copy-start
  6.5 0.0 all-gather.2.cloned.1.call-start
  6.5 0.7 all-gather.2.cloned.1.call-update
  7.3 3.3 copy.21
  10.5 8.1 %copy.22 = bf16[256,64,64]{1,2,0:T(8,128)(2,1)} copy(bf16[256,64,64]{0,2,1:T(8,128)(2,1)S(1)} %bitcast.63) | data formatting | bytes 4194304 | tf_op jit(solution)/shard_map/reshape;squeeze | solution.py:34
  18.6 0.7 dynamic-slice_reduce_fusion
  19.3 0.1 reshape.166
  19.4 0.7 fusion.15
  20.1 0.7 and_bitcast_fusion
  20.8 0.7 compare_and_fusion.1
  21.5 0.7 compare_select_fusion.1
  22.3 0.1 broadcast_subtract_fusion
  22.4 91.7 %all-gather.2.cloned.1.call-done = bf16[2048,1792]{1,0:T(8,128)(2,1)} async-done(((bf16[64,1792]{1,0:T(8,128)(2,1)}), bf16[2048,1792]{1,0:T(8,128)(2,1)}) %all-gather.2.cloned.1.call-update) | async-done | bytes 7340048 | tf_op jit(solution)/shard_map/all_gather | solution.py:21
  114.0 5.4 %gather_fusion = bf16[128,1792]{1,0:T(8,128)(2,1)S(1)} fusion(bf16[2048,1792]{1,0:T(8,128)(2,1)} %all-gather.2.cloned.1.call-done, s32[1024]{0:T(1024)S(1)} %pad_clamp_fusion.1), kind=kCustom, calls=%fused_computation | custom fusion | bytes 918016 | tf_op jit(solution)/shard_map/jit(_take)/gather | solution.py:25
  119.4 0.3 copy.20
  119.7 0.1 select_select_fusion
  119.7 3.1 gather_fusion.1
  122.9 4.8 %fusion.2 = f32[256,128,64]{1,2,0:T(8,128)S(1)} fusion(bf16[256,64,64]{1,2,0:T(8,128)(2,1)} %copy.22, bf16[256,128,64]{1,2,0:T(8,128)(2,1)} %gather_fusion.1, pred[256]{0:T(512)(128)(4,1)S(1)} %compare_and_fusion.2), kind=kOutput, calls=%fused_computation.6 | convolution fusion | flops 270532608 | bytes 14680320 | tf_op jit(solution)/shard_map/tnb,nbc->tnc/dot_general | solution.py:38
  127.7 7.6 %convert_bitcast_fusion.1 = bf16[128,32,4,64]{0,2,3,1:T(4,128)(2,1)S(1)} fusion(f32[128,32,8,64]{0,3,2,1:T(8,128)S(1)} %bitcast.58, s32[32,8]{1,0:T(8,128)S(1)} %broadcast_subtract_fusion), kind=kOutput, calls=%fused_computation.12 | convolution fusion | flops 101712896 | bytes 10486784 | tf_op jit(solution)/shard_map/tgbx,gbc->tgcx/dot_general | solution.py:45
  135.2 0.5 copy.24
  135.8 33.5 %copy.37 = bf16[1,128,8192]{1,0,2:T(2,128)(2,1)} copy(bf16[1,128,8192]{1,2,0:T(8,128)(2,1)S(1)} %bitcast.62) | data formatting | bytes 4194304 | tf_op jit(solution)/shard_map/convert_element_type | solution.py:47
  169.2 0.5 broadcast.189
  169.7 45.2 %reduce.4 = bf16[8192,128]{1,0:T(8,128)(2,1)S(1)} reduce(bf16[8192,1,128]{2,1,0:T(2,128)(2,1)} %bitcast.59, bf16[]{:T(256)} %broadcast.189), dimensions={1}, to_apply=%bitcast.55.reduce_sub_computation | reduce | bytes 4194306
  214.9 0.0 copy-start.1
  214.9 2.1 reshape.203
  217.1 5.5 %all-to-all-start = ((bf16[32,2,16384]{2,1,0:T(2,128)(2,1)}), bf16[32,2,16384]{2,1,0:T(2,128)(2,1)S(1)}, u32[]{:S(2)}, u32[]{:S(2)}) async-start(bf16[32,2,16384]{2,1,0:T(2,128)(2,1)} %reshape.203), calls=%async_computation | async-start | bytes 4194304 | tf_op jit(solution)/shard_map/all_to_all | solution.py:46
  222.6 0.0 reduce-scatter.2.cloned.1.call-start
  222.6 0.0 copy-done.1
  222.6 9.3 %reduce-window.6 = s32[32,16,128]{2,1,0:T(8,128)S(1)} reduce-window(s32[32,16,128]{2,1,0:T(8,128)S(1)} %fusion.11, s32[]{:T(128)} %constant.104.clone.1), window={size=1x1x128 pad=0_0x0_0x127_0}, to_apply=%region_0.1 | reduce-window | flops 8323072 | bytes 524292 | tf_op jit(solution)/shard_map/reduce-window
  231.9 0.1 slice.14
  232.1 0.9 copy.29
  232.9 0.9 reduce-window.9
  233.8 0.1 add_add_fusion
  234.0 0.1 fusion.10
  234.1 36.5 %all-to-all-done = bf16[32,2,16384]{2,1,0:T(2,128)(2,1)S(1)} async-done(((bf16[32,2,16384]{2,1,0:T(2,128)(2,1)}), bf16[32,2,16384]{2,1,0:T(2,128)(2,1)S(1)}, u32[]{:S(2)}, u32[]{:S(2)}) %all-to-all-start) | async-done | bytes 2097184 | tf_op jit(solution)/shard_map/all_to_all | solution.py:46
  270.7 6.8 %reshape.204 = bf16[8192,1,128]{2,1,0:T(2,128)(2,1)} reshape(bf16[32,2,16384]{2,1,0:T(2,128)(2,1)S(1)} %all-to-all-done) | data formatting | bytes 4194304
  277.4 2.5 copy.26
  279.9 2.6 convert_bitcast_fusion
  282.5 5.6 %copy.27 = f32[32,1,128,256]{3,2,0,1:T(8,128)} copy(f32[32,1,128,256]{2,3,0,1:T(8,128)} %convert_bitcast_fusion) | data formatting | bytes 8388608 | tf_op jit(solution)/shard_map/convert_element_type | solution.py:52
  288.1 8.8 %gather_fusion.2 = f32[2048,256]{1,0:T(8,128)S(1)} fusion(f32[4096,256]{1,0:T(8,128)} %bitcast.57, s32[2048]{0:T(1024)S(1)} %broadcast_clamp_fusion), kind=kCustom, calls=%fused_computation.2 | custom fusion | bytes 4202496 | tf_op jit(solution)/shard_map/jit(_take)/gather | solution.py:57
  296.9 0.0 copy-done
  296.9 6.5 %convolution_add_fusion = f32[2048,256]{1,0:T(8,128)} fusion(bf16[2048,1792]{1,0:T(8,128)(2,1)} %all-gather.2.cloned.1.call-done, bf16[1792,256]{1,0:T(8,128)(2,1)S(1)} %copy-done, f32[2048,256]{1,0:T(8,128)S(1)} %gather_fusion.2, pred[2048]{0:T(1024)(128)(4,1)S(1)} %compare_and_fusion), kind=kOutput, calls=%fused_computation.10 | convolution fusion | flops 1880096768 | bytes 12453888 | tf_op jit(solution)/shard_map/dot_general | solution.py:26
  303.5 0.0 reduce-scatter.2.cloned.1.call-update
  303.5 59.9 %reduce-scatter.2.cloned.1.call-done = f32[128,256]{1,0:T(8,128)} async-done(((f32[2048,256]{1,0:T(8,128)}), f32[128,256]{1,0:T(8,128)}) %reduce-scatter.2.cloned.1.call-update) | async-done | bytes 131088 | tf_op jit(solution)/shard_map/reduce_scatter | solution.py:59
  363.4 1.5 convert_element_type.47
  (7 shorter events, 0.1 us)
Async XLA Ops:
  6.5 290.4 %copy-start = (bf16[1792,256]{1,0:T(8,128)(2,1)S(1)}, bf16[1792,256]{1,0:T(8,128)(2,1)}, u32[]{:S(2)}) copy-start(bf16[1792,256]{1,0:T(8,128)(2,1)} %param.8) | copy-start | bytes 2752516
  6.5 107.5 %all-gather.2.cloned.1.call-start = ((), (), s32[]{:S(2)}) async-start(), calls=%async_computation.2 | async-start | bytes 7569408 | tf_op jit(solution)/shard_map/all_gather | solution.py:21
  214.9 7.7 %copy-start.1 = (s32[2048]{0:T(1024)S(1)}, s32[2048]{0:T(1024)}, u32[]{:S(2)}) copy-start(s32[2048]{0:T(1024)} %param.12) | copy-start | bytes 24580
  217.1 53.6 %all-to-all-start = ((bf16[32,2,16384]{2,1,0:T(2,128)(2,1)}), bf16[32,2,16384]{2,1,0:T(2,128)(2,1)S(1)}, u32[]{:S(2)}, u32[]{:S(2)}) async-start(bf16[32,2,16384]{2,1,0:T(2,128)(2,1)} %reshape.203), calls=%async_computation | async-start | bytes 4194304 | tf_op jit(solution)/shard_map/all_to_all | solution.py:46
  222.6 140.8 %reduce-scatter.2.cloned.1.call-start = ((), (), s32[]{:S(2)}) async-start(), calls=%async_computation.3 | async-start | bytes 2228224 | tf_op jit(solution)/shard_map/reduce_scatter | solution.py:59
Sparse Core Ops, SparseCore 0:
  10.5 103.4 all-gather.1
  303.6 59.7 reduce-scatter.1
where the time goes:
time: 375 us; the launch traced here: 372 us
  waiting for transfers between devices  189 us (50%)
  local copies, waits for them, and re-layouts  82.2 us (22%)
  other arithmetic  62.7 us (17%)
  matrix products  18.9 us (5%)
  between operations  13.6 us (4%)
  starting transfers between devices  5.54 us (1%)
    all_gather x1, waiting for transfers between devices, per_device(): piece = lax.all_gather(hidden, 'seq', axis=0, tiled=True)  91.7 us
    reduce_scatter x1, waiting for transfers between devices, per_device(): lax.psum_scatter(total, 'tensor', scatter_dimension=0, tiled=True)  59.9 us
    unnamed x1, other arithmetic  45.2 us
    all_to_all x1, waiting for transfers between devices, per_device(): lax.all_to_all(placed.reshape(1, capacity, seq_count * width_local).astyp...  36.5 us
    convert_element_type x2, local copies, waits for them, and re-layouts, per_device(): placed.reshape(1, capacity, seq_count * width_local).astype(jnp.bfloat16)  34 us
    unnamed x8, local copies, waits for them, and re-layouts  12.7 us
    another operation x2, other arithmetic  10.2 us
    gather x1, local copies, waits for them, and re-layouts, per_device(): delta_rows = jnp.take(flat, tenant_ids * capacity + rank, axis=0)  8.83 us
  transfers between devices with their start and end apart: 3, of which 3 were waited for; matrix products, arithmetic and copies ran while one was open for 7% of the time, Pallas kernels for 0%

commit v1 on v0

v1 whole, which is shorter than its diff:
```python
import jax
import jax.numpy as jnp
from jax import lax
from jax.experimental import pallas as pl
from jax.experimental.pallas import tpu as pltpu
from jax.sharding import Mesh, PartitionSpec as P

BLK = 64
LANES = 128
SEQ = ("y", "x")
TENSOR = ("z", "core")
CORE_SWAP = [(0, 1), (1, 0)]


def delta_kernel(rows, cols, own_rows, other_rows, own_blocks, other_blocks, out, table):
    group = pl.program_id(0)
    per_group, half_rows, _ = own_blocks.shape
    tiles = own_rows.shape[1] // LANES
    low = lax.broadcasted_iota(jnp.int32, (1, LANES), 1) < BLK
    low_f = low.astype(jnp.float32).astype(jnp.bfloat16)
    high_f = (~low).astype(jnp.float32).astype(jnp.bfloat16)

    @pl.when(group == 0)
    def _():
        source = lax.broadcasted_iota(jnp.int32, (LANES, 2 * LANES), 0)
        place = lax.broadcasted_iota(jnp.int32, (LANES, 2 * LANES), 1)
        copy, lane = place // LANES, place % LANES
        half = (lane // BLK) ^ copy
        inner = lane % BLK
        wanted = half * BLK + (inner % (BLK // 2)) * 2 + inner // (BLK // 2)
        order = (source == wanted).astype(jnp.float32).astype(jnp.bfloat16)
        for side, ref in enumerate((own_rows, other_rows)):
            for tile in range(tiles):
                both = jnp.dot(
                    ref[:, tile * LANES : (tile + 1) * LANES], order, preferred_element_type=jnp.float32
                ).astype(jnp.bfloat16)
                table[(side * 2) * tiles + tile] = both[:, :LANES]
                table[(side * 2 + 1) * tiles + tile] = both[:, LANES:]

    lane_col = lax.broadcasted_iota(jnp.int32, (1, LANES), 1) // BLK
    pieces, weights = [], []
    for side, blocks in enumerate((own_blocks, other_blocks)):
        for pair in range(per_group // 2):
            picked = []
            for position in range(2):
                n = pair * 2 + position
                slot = group * per_group + n
                row = jnp.maximum(rows[side, slot], 0)
                swapped = (row & 1) ^ position
                picked.append(table[(side * 2 + swapped) * tiles + row // 2])
                column = cols[side, slot]
                column = jnp.where(column >= 0, column & 3, -1)
                block = blocks[n]
                turned = pltpu.roll(block.astype(jnp.float32), BLK, 1).astype(jnp.bfloat16)
                evens = block * low_f + turned * high_f
                odds = turned * low_f + block * high_f
                first = (lane_col == column).astype(jnp.float32).astype(jnp.bfloat16)
                second = (lane_col + 2 == column).astype(jnp.float32).astype(jnp.bfloat16)
                weights.append(jnp.concatenate([evens * first, evens * second], axis=1))
                weights.append(jnp.concatenate([odds * first, odds * second], axis=1))
            pieces.append(picked[0] * low_f + picked[1] * high_f)
    left = jnp.concatenate(pieces, axis=1)
    right = jnp.concatenate(weights, axis=0)
    out[0] = jnp.dot(left, right, preferred_element_type=jnp.float32).astype(out.dtype)


def delta_products(rows, cols, own_rows, other_rows, own_blocks, other_blocks, groups, width):
    count, ff = own_rows.shape
    slots, half_rows, lanes = own_blocks.shape
    per_group = slots // groups
    fixed = pl.BlockSpec((count, ff), lambda g, *_: (0, 0))
    blocks = pl.BlockSpec((per_group, half_rows, lanes), lambda g, *_: (g, 0, 0))
    return pl.pallas_call(
        delta_kernel,
        grid_spec=pltpu.PrefetchScalarGridSpec(
            num_scalar_prefetch=2,
            grid=(groups,),
            in_specs=[fixed, fixed, blocks, blocks],
            out_specs=pl.BlockSpec((1, count, width), lambda g, *_: (g, 0, 0)),
            scratch_shapes=[pltpu.VMEM((4 * ff // LANES, count, LANES), jnp.bfloat16)],
        ),
        out_shape=jax.ShapeDtypeStruct((groups, count, width), jnp.bfloat16),
        compiler_params=pltpu.CompilerParams(vmem_limit_bytes=24 * 2**20),
    )(rows, cols, own_rows, other_rows, own_blocks, other_blocks)


def place_kernel(core, tokens, rows, base, out):
    tile = pl.program_id(0) * 2 + pl.program_id(1)
    count = base.shape[0]
    token = lax.broadcasted_iota(jnp.int32, (count, 1), 0) + tile * count
    hot = (tokens[...] == token).astype(jnp.float32).astype(jnp.bfloat16)
    moved = jnp.dot(hot, rows[...], preferred_element_type=jnp.float32)
    out[0, 0] = (moved + base[...]).astype(out.dtype)


def place_rows(core, tokens, rows, base, planes):
    total, width = base.shape
    count = total // planes // 2
    return pl.pallas_call(
        place_kernel,
        grid_spec=pltpu.PrefetchScalarGridSpec(
            num_scalar_prefetch=1,
            grid=(planes, 2),
            in_specs=[
                pl.BlockSpec((1, tokens.shape[1]), lambda z, c, core: (0, 0)),
                pl.BlockSpec(rows.shape, lambda z, c, core: (0, 0)),
                pl.BlockSpec((count, width), lambda z, c, core: (z * 2 + c, 0)),
            ],
            out_specs=pl.BlockSpec((1, 1, count, width), lambda z, c, core: (c ^ core[0], z, 0, 0)),
        ),
        out_shape=jax.ShapeDtypeStruct((2, planes, count, width), jnp.bfloat16),
        compiler_params=pltpu.CompilerParams(vmem_limit_bytes=24 * 2**20),
    )(core, tokens, rows, base)


def per_device(hidden, down_weight, delta_blocks, block_rows, block_cols, tenant_ids, tenant_lists):
    core = lax.axis_index("core")
    seq_index = lax.axis_index(SEQ)
    tensor_index = lax.axis_index(TENSOR)
    seq_count = lax.axis_size(SEQ)
    planes = lax.axis_size("z")
    variants, capacity = tenant_lists.shape
    half = capacity // 2
    ff_local, width = down_weight.shape
    slots = delta_blocks.shape[1]

    own_blocks = delta_blocks[0].reshape(slots, BLK // 2, 2 * BLK)
    other_blocks = lax.ppermute(own_blocks, "core", CORE_SWAP)
    pair = jnp.stack([tensor_index, tensor_index ^ 1])
    rows = lax.dynamic_index_in_dim(block_rows, seq_index, 0, False)[pair]
    cols = lax.dynamic_index_in_dim(block_cols, seq_index, 0, False)[pair]

    gathered = lax.all_gather(hidden, SEQ, axis=0, tiled=True)
    tokens = gathered.shape[0]
    own_list = lax.dynamic_index_in_dim(tenant_lists, seq_index, 0, False).reshape(2, half)
    ordered = jnp.stack([own_list[core], own_list[1 - core]]).reshape(capacity)
    hot = (ordered[:, None] == jnp.arange(tokens, dtype=jnp.int32)[None, :]).astype(jnp.bfloat16)
    picked = jnp.dot(hot, gathered, preferred_element_type=jnp.float32).astype(jnp.bfloat16)
    other_picked = lax.ppermute(picked[half:], "core", CORE_SWAP)
    delta = delta_products(rows, cols, picked[:half], other_picked, own_blocks, other_blocks, seq_count, width)
    received = lax.all_to_all(delta, SEQ, split_axis=0, concat_axis=0, tiled=True)
    base = jnp.dot(gathered, down_weight, preferred_element_type=jnp.float32)
    lists = tenant_lists.reshape(variants, 2, half)
    held = lax.dynamic_index_in_dim(lists, core, 1, False).reshape(1, variants * half)
    partial = place_rows(core.reshape(1).astype(jnp.int32), held, received.reshape(variants * half, width), base, planes)
    swapped = lax.ppermute(partial[1], "core", CORE_SWAP)
    summed = (partial[0].astype(jnp.float32) + swapped.astype(jnp.float32)).astype(jnp.bfloat16)
    parts = lax.all_to_all(summed, "z", split_axis=0, concat_axis=0, tiled=True)
    return jnp.sum(parts.astype(jnp.float32), axis=0).astype(jnp.bfloat16)


def solution(mesh):
    fine = Mesh(mesh.devices.reshape(8, 4, 8, 2), ("y", "x", "z", "core"))
    return jax.shard_map(
        per_device,
        mesh=fine,
        in_specs=(
            P(SEQ, TENSOR),
            P(TENSOR, SEQ),
            P(SEQ, TENSOR, None),
            P(),
            P(),
            P(),
            P(),
        ),
        out_specs=P(TENSOR, SEQ),
        check_vma=False,
    )
```

time: 375 us -> 225 us (0.60)
  local copies, waits for them, and re-layouts: 82.2 us -> 10.5 us
  waiting for transfers between devices: 189 us -> 118 us
  other arithmetic: 62.7 us -> 0.93 us
  Pallas kernels: 0 us -> 25.3 us
  blocking collectives: 0 us -> 23.6 us
  starting transfers between devices: 5.54 us -> 20.9 us
  matrix products: 18.9 us -> 10.8 us
    reduce_scatter x1 -> x0, waiting for transfers between devices: 59.9 us -> none  [per_device(): lax.psum_scatter(total, 'tensor', scatter_dimension=0, tiled=True)]
    unnamed x1 -> x0, other arithmetic: 45.2 us -> none
    convert_element_type x3 -> x0, local copies, waits for them, and re-layouts: 39.6 us -> none  [the longest x2 34 us: per_device(): placed.reshape(1, capacity, seq_count * width_local).astype(jnp.bfloat16)]
    pallas_call x0 -> x2, Pallas kernels: none -> 25.3 us  [the longest x1 20.2 us: delta_products(): pl.pallas_call(delta_kernel, grid_spec=pltpu.PrefetchScalarGridSpec(num_s...]
    all_to_all x0 -> x1, blocking collectives: none -> 23.6 us  [per_device(): parts = lax.all_to_all(summed, 'z', split_axis=0, concat_axis=0, tiled=True)]
    gather x4 -> x2, local copies, waits for them, and re-layouts: 17.6 us -> 1.12 us  [the longest x1 0.56 us: per_device(): rows = lax.dynamic_index_in_dim(block_rows, seq_index, 0, False)[pair]]
    all_to_all x1, waiting for transfers between devices: 36.5 us -> 20.5 us  [per_device(): lax.all_to_all(delta, SEQ, split_axis=0, concat_axis=0, tiled=True)]
    ppermute x0 -> x3, starting transfers between devices: none -> 15.4 us  [the longest x1 8.79 us: per_device(): other_blocks = lax.ppermute(own_blocks, 'core', CORE_SWAP)]
  transfers between devices with their start and end apart: 3 -> 5, of which waited for: 3 -> 3; matrix products, arithmetic and copies ran while one was open for 7% -> 7% of each run, Pallas kernels for 0% -> 0%
where the time goes in v1:
time: 225 us; the launch traced here: 223 us
  waiting for transfers between devices  118 us (52%)
  Pallas kernels  25.3 us (11%)
  blocking collectives  23.6 us (10%)
  starting transfers between devices  20.9 us (9%)
  between operations  13.5 us (6%)
  matrix products  10.8 us (5%)
  local copies, waits for them, and re-layouts  10.5 us (5%)
    all_gather x1, waiting for transfers between devices, per_device(): gathered = lax.all_gather(hidden, SEQ, axis=0, tiled=True)  95 us
    all_to_all x1, blocking collectives, per_device(): parts = lax.all_to_all(summed, 'z', split_axis=0, concat_axis=0, tiled=True)  23.6 us
    all_to_all x1, waiting for transfers between devices, per_device(): lax.all_to_all(delta, SEQ, split_axis=0, concat_axis=0, tiled=True)  20.5 us
    pallas_call x1, Pallas kernels, delta_products(): pl.pallas_call(delta_kernel, grid_spec=pltpu.PrefetchScalarGridSpec(num_s...  20.2 us
    ppermute x1, starting transfers between devices, per_device(): other_blocks = lax.ppermute(own_blocks, 'core', CORE_SWAP)  8.79 us
    unnamed x13, local copies, waits for them, and re-layouts  6.81 us
    dot_general x1, matrix products, per_device(): base = jnp.dot(gathered, down_weight, preferred_element_type=jnp.float32)  6.56 us
    all_to_all x1, starting transfers between devices, per_device(): lax.all_to_all(delta, SEQ, split_axis=0, concat_axis=0, tiled=True)  5.49 us
  transfers between devices with their start and end apart: 5, of which 3 were waited for; matrix products, arithmetic and copies ran while one was open for 7% of the time, Pallas kernels for 0%

profile of v1, /device:TPU:1, one launch (start us, length us, event | category | flops | bytes accessed | tf_op | source)
XLA Modules:
  0.0 223.3 jit_solution(2270679387607857516)
XLA Ops:
  6.5 0.0 copy-start
  6.5 0.0 all-gather.2.cloned.1.call-start
  6.5 0.7 all-gather.2.cloned.1.call-update
  7.3 2.1 copy.9
  9.3 8.8 %collective-permute-start.1 = (bf16[256,32,128]{2,1,0:T(8,128)(2,1)S(1)}, bf16[256,32,128]{2,1,0:T(8,128)(2,1)}, u32[]{:S(2)}, u32[]{:S(2)}) collective-permute-start(bf16[256,32,128]{2,1,0:T(8,128)(2,1)S(1)} %bitcast.26), channel_id=1, source_target_pairs={{0,1},{1,0},{2,3},{3,2},{4,5},{5,4},{6,7},{7,6},{8,9},{9,8},{10,11... | collective-permute-start | bytes 6291464 | tf_op jit(solution)/shard_map/ppermute | solution.py:128
  18.1 0.7 fusion.2
  18.9 0.1 reshape.108
  19.0 0.1 eq.15
  19.0 95.0 %all-gather.2.cloned.1.call-done = bf16[2048,1792]{1,0:T(8,128)(2,1)} async-done(((bf16[64,1792]{1,0:T(8,128)(2,1)}), bf16[2048,1792]{1,0:T(8,128)(2,1)}) %all-gather.2.cloned.1.call-update) | async-done | bytes 7340048 | tf_op jit(solution)/shard_map/all_gather | solution.py:133
  114.0 4.3 %convolution_convert_fusion = bf16[128,1792]{1,0:T(8,128)(2,1)S(1)} fusion(bf16[2048,1792]{1,0:T(8,128)(2,1)} %all-gather.2.cloned.1.call-done, s32[128]{0:T(128)S(1)} %eq.15), kind=kOutput, calls=%fused_computation.2 | convolution fusion | flops 940015616 | bytes 7799296 | tf_op jit(solution)/shard_map/dot_general | solution.py:138
  118.3 0.0 copy-start.5
  118.3 0.7 fusion.4
  119.0 3.0 %collective-permute-start = (bf16[64,1792]{1,0:T(8,128)(2,1)}, bf16[64,1792]{1,0:T(8,128)(2,1)S(1)}, u32[]{:S(2)}, u32[]{:S(2)}) collective-permute-start(bf16[64,1792]{1,0:T(8,128)(2,1)} %get-tuple-element.5), channel_id=1, source_target_pairs={{0,1},{1,0},{2,3},{3,2},{4,5},{5,4},{6,7},{7,6},{8,9},{9,8},{10,11... | collective-permute-start | bytes 688136 | tf_op jit(solution)/shard_map/ppermute | solution.py:139
  122.0 0.1 fusion.3
  122.1 0.7 dynamic-slice_bitcast_fusion
  122.8 0.6 gather_fusion.1
  123.4 0.6 gather_fusion
  124.0 0.0 collective-permute-done.1.other_blocks
  124.0 0.0 collective-permute-done.other_rows
  124.0 20.2 %shard_map.64 = bf16[32,64,256]{2,1,0:T(8,128)(2,1)S(1)} custom-call(s32[2,256]{1,0:T(2,128)S(1)} %gather_fusion, s32[2,256]{1,0:T(2,128)S(1)} %gather_fusion.1, bf16[64,1792]{1,0:T(8,128)(2,1)S(1)} %get-tuple-element.6.own_rows, bf16[64,1792]{1,0:T(8,128)(2,1)S(1)} %collective-permute-done.other_rows, bf16[256,32,128]{2,1,0:T(8,128)(2,1)S(1)} %bitcast.27, ...), custom_call_target="tpu_custom_call" | custom-call | tf_op jit(solution)/shard_map/pallas_call | solution.py:73
  144.2 0.0 copy-start.1
  144.2 0.9 copy-done.1
  145.2 5.5 %all-to-all-start = ((bf16[32,64,256]{2,1,0:T(8,128)(2,1)}), bf16[32,64,256]{2,1,0:T(8,128)(2,1)S(1)}, u32[]{:S(2)}, u32[]{:S(2)}) async-start(bf16[32,64,256]{2,1,0:T(8,128)(2,1)} %copy-done.1), calls=%async_computation | async-start | bytes 2097152 | tf_op jit(solution)/shard_map/all_to_all | solution.py:141
  150.7 0.0 copy-done.5
  150.7 0.1 reshape.106
  150.8 0.1 reshape.107.tokens
  150.9 0.0 copy-done
  150.9 6.6 %fusion.5.base = f32[2048,256]{1,0:T(8,128)} fusion(bf16[2048,1792]{1,0:T(8,128)(2,1)} %all-gather.2.cloned.1.call-done, bf16[1792,256]{1,0:T(8,128)(2,1)S(1)} %copy-done), kind=kOutput, calls=%fused_computation.21 | convolution fusion | flops 1879048192 | bytes 10354688 | tf_op jit(solution)/shard_map/dot_general | solution.py:142
  157.4 20.5 %all-to-all-done = bf16[32,64,256]{2,1,0:T(8,128)(2,1)S(1)} async-done(((bf16[32,64,256]{2,1,0:T(8,128)(2,1)}), bf16[32,64,256]{2,1,0:T(8,128)(2,1)S(1)}, u32[]{:S(2)}, u32[]{:S(2)}) %all-to-all-start) | async-done | bytes 1048608 | tf_op jit(solution)/shard_map/all_to_all | solution.py:141
  177.9 0.0 copy-start.2
  177.9 1.0 copy-done.2
  178.9 0.0 copy-start.3
  178.9 1.2 copy-done.3
  180.1 0.0 copy-start.4
  180.1 1.6 copy-done.4
  181.7 5.0 %shard_map.65 = bf16[2,8,128,256]{3,2,1,0:T(8,128)(2,1)S(1)} custom-call(s32[1]{0:T(128)} %bitcast.core, s32[1,2048]{1,0:T(1,128)S(1)} %reshape.107.tokens, bf16[2048,256]{1,0:T(8,128)(2,1)S(1)} %bitcast.28, f32[2048,256]{1,0:T(8,128)S(1)} %copy-done.4), custom_call_target="tpu_custom_call" | custom-call | tf_op jit(solution)/shard_map/pallas_call | solution.py:99
  186.8 3.7 %collective-permute-start.2 = (bf16[8,128,256]{2,1,0:T(8,128)(2,1)S(1)}, bf16[8,128,256]{2,1,0:T(8,128)(2,1)S(1)}, u32[]{:S(2)}, u32[]{:S(2)}) collective-permute-start(bf16[8,128,256]{2,1,0:T(8,128)(2,1)S(1)} %slice_bitcast_fusion), channel_id=1, source_target_pairs={{0,1},{1,0},{2,3},{3,2},{4,5},{5,4},{6,7},{7,6},{8,9},{9,8},{10,11... | collective-permute-start | bytes 1572872 | tf_op jit(solution)/shard_map/ppermute | solution.py:146
  190.5 1.5 collective-permute-done.2
  192.0 0.1 fusion
  192.1 23.6 %all_to_all.10 = bf16[8,128,256]{2,1,0:T(8,128)(2,1)S(1)} all-to-all(bf16[8,128,256]{2,1,0:T(8,128)(2,1)S(1)} %fusion), channel_id=1, replica_groups=mesh['y'=8,'x'=4,'z'=8,'core'=2] {'z'}, dimensions={0} | all-to-all | bytes 1048576 | tf_op jit(solution)/shard_map/all_to_all | solution.py:148
  215.7 0.7 reduce_sum.12
  (5 shorter events, 0.1 us)
Async XLA Ops:
  6.5 144.3 %copy-start = (bf16[1792,256]{1,0:T(8,128)(2,1)S(1)}, bf16[1792,256]{1,0:T(8,128)(2,1)}, u32[]{:S(2)}) copy-start(bf16[1792,256]{1,0:T(8,128)(2,1)} %param.8) | copy-start | bytes 2752516
  6.5 107.5 %all-gather.2.cloned.1.call-start = ((), (), s32[]{:S(2)}) async-start(), calls=%async_computation.2 | async-start | bytes 7569408 | tf_op jit(solution)/shard_map/all_gather | solution.py:133
  9.3 114.6 %collective-permute-start.1 = (bf16[256,32,128]{2,1,0:T(8,128)(2,1)S(1)}, bf16[256,32,128]{2,1,0:T(8,128)(2,1)}, u32[]{:S(2)}, u32[]{:S(2)}) collective-permute-start(bf16[256,32,128]{2,1,0:T(8,128)(2,1)S(1)} %bitcast.26), channel_id=1, source_target_pairs={{0,1},{1,0},{2,3},{3,2},{4,5},{5,4},{6,7},{7,6},{8,9},{9,8},{10,11... | collective-permute-start | bytes 6291464 | tf_op jit(solution)/shard_map/ppermute | solution.py:128
  118.3 32.4 %copy-start.5 = (s32[32,128]{1,0:T(8,128)S(1)}, s32[32,128]{1,0:T(8,128)}, u32[]{:S(2)}) copy-start(s32[32,128]{1,0:T(8,128)} %param.12) | copy-start | bytes 49156
  119.0 4.9 %collective-permute-start = (bf16[64,1792]{1,0:T(8,128)(2,1)}, bf16[64,1792]{1,0:T(8,128)(2,1)S(1)}, u32[]{:S(2)}, u32[]{:S(2)}) collective-permute-start(bf16[64,1792]{1,0:T(8,128)(2,1)} %get-tuple-element.5), channel_id=1, source_target_pairs={{0,1},{1,0},{2,3},{3,2},{4,5},{5,4},{6,7},{7,6},{8,9},{9,8},{10,11... | collective-permute-start | bytes 688136 | tf_op jit(solution)/shard_map/ppermute | solution.py:139
  144.2 1.0 copy-start.1
  145.2 32.8 %all-to-all-start = ((bf16[32,64,256]{2,1,0:T(8,128)(2,1)}), bf16[32,64,256]{2,1,0:T(8,128)(2,1)S(1)}, u32[]{:S(2)}, u32[]{:S(2)}) async-start(bf16[32,64,256]{2,1,0:T(8,128)(2,1)} %copy-done.1), calls=%async_computation | async-start | bytes 2097152 | tf_op jit(solution)/shard_map/all_to_all | solution.py:141
  177.9 1.0 copy-start.2
  178.9 1.2 copy-start.3
  180.1 1.6 copy-start.4
  186.8 5.2 %collective-permute-start.2 = (bf16[8,128,256]{2,1,0:T(8,128)(2,1)S(1)}, bf16[8,128,256]{2,1,0:T(8,128)(2,1)S(1)}, u32[]{:S(2)}, u32[]{:S(2)}) collective-permute-start(bf16[8,128,256]{2,1,0:T(8,128)(2,1)S(1)} %slice_bitcast_fusion), channel_id=1, source_target_pairs={{0,1},{1,0},{2,3},{3,2},{4,5},{5,4},{6,7},{7,6},{8,9},{9,8},{10,11... | collective-permute-start | bytes 1572872 | tf_op jit(solution)/shard_map/ppermute | solution.py:146
Sparse Core Ops, SparseCore 0:
  10.5 103.4 all-gather.1

commit v2 on v1

v2 whole, which is shorter than its diff:
```python
import jax
import jax.numpy as jnp
from jax import lax
from jax.experimental import pallas as pl
from jax.experimental.pallas import tpu as pltpu
from jax.sharding import Mesh, PartitionSpec as P

BLK = 64
LANES = 128
SEQ = ("y", "x")
TENSOR = ("z", "core")
CHIPS = ("x", "core")
CORE_SWAP = [(0, 1), (1, 0)]
STEP_GROUPS = 2
SPREAD_GROUPS = 4


def as_bf16(mask):
    return mask.astype(jnp.float32).astype(jnp.bfloat16)


def spread_kernel(core, own, other, lists, tokens, out, hot):
    low = lax.broadcasted_iota(jnp.int32, (1, LANES), 1) < BLK
    low_f, high_f = as_bf16(low), as_bf16(~low)
    hot[...] = as_bf16(lists[...] == tokens[...])

    def spread(blocks):
        for n in range(blocks.shape[0]):
            block = blocks[n]
            turned = pltpu.roll(block.astype(jnp.float32), BLK, 1).astype(jnp.bfloat16)
            out[0, n, : BLK // 2] = block * low_f + turned * high_f
            out[0, n, BLK // 2 :] = turned * low_f + block * high_f

    pl.when(pl.program_id(0) == 0)(lambda: spread(own))
    pl.when(pl.program_id(0) == 1)(lambda: spread(other))


def spread_blocks(core, own, other, lists, tokens, groups):
    slots, half_rows, lanes = own.shape
    steps = groups // SPREAD_GROUPS
    count = slots // steps
    picks = lists.shape[0]
    return pl.pallas_call(
        spread_kernel,
        grid_spec=pltpu.PrefetchScalarGridSpec(
            num_scalar_prefetch=1,
            grid=(2, steps),
            in_specs=[
                pl.BlockSpec((count, half_rows, lanes), lambda s, g, *_: (g * (1 - s) + (steps - 1) * s, 0, 0)),
                pl.BlockSpec((count, half_rows, lanes), lambda s, g, *_: (g * s, 0, 0)),
                pl.BlockSpec((picks // steps, 1), lambda s, g, *_: (g, 0)),
                pl.BlockSpec(tokens.shape, lambda s, g, *_: (0, 0)),
            ],
            out_specs=[
                pl.BlockSpec((1, count, BLK, LANES), lambda s, g, core: (s ^ core[0], g, 0, 0)),
                pl.BlockSpec((picks // steps, tokens.shape[1]), lambda s, g, *_: (g, 0)),
            ],
        ),
        out_shape=[
            jax.ShapeDtypeStruct((2, slots, BLK, LANES), jnp.bfloat16),
            jax.ShapeDtypeStruct((picks, tokens.shape[1]), jnp.bfloat16),
        ],
        compiler_params=pltpu.CompilerParams(vmem_limit_bytes=16 * 2**20),
        cost_estimate=pl.CostEstimate(flops=0, bytes_accessed=40_000_000, transcendentals=0),
    )(core, own, other, lists, tokens)


def delta_kernel(rows, cols, *refs):
    *sent, weights, out, table = refs
    step = pl.program_id(0)
    per_group = weights.shape[1] // STEP_GROUPS
    tiles = sum(ref.shape[2] for ref in sent) // LANES
    lane_col = lax.broadcasted_iota(jnp.int32, (1, LANES), 1) // BLK
    low_f, high_f = as_bf16(lane_col == 0), as_bf16(lane_col == 1)

    @pl.when(step == 0)
    def _():
        source = lax.broadcasted_iota(jnp.int32, (LANES, 2 * LANES), 0)
        place = lax.broadcasted_iota(jnp.int32, (LANES, 2 * LANES), 1)
        copy, lane = place // LANES, place % LANES
        half = (lane // BLK) ^ copy
        inner = lane % BLK
        wanted = half * BLK + (inner % (BLK // 2)) * 2 + inner // (BLK // 2)
        order = as_bf16(source == wanted)
        for side in range(2):
            tile = 0
            for ref in sent:
                for at in range(0, ref.shape[2], LANES):
                    mine = ref[side, :, at : at + LANES]
                    for x in range(1, ref.shape[0] // 2):
                        mine = mine + ref[2 * x + side, :, at : at + LANES]
                    both = jnp.dot(mine, order, preferred_element_type=jnp.float32).astype(jnp.bfloat16)
                    table[(side * 2) * tiles + tile] = both[:, :LANES]
                    table[(side * 2 + 1) * tiles + tile] = both[:, LANES:]
                    tile += 1

    for inner in range(STEP_GROUPS):
        total = None
        for side in range(2):
            pieces, spread = [], []
            for pair in range(per_group // 2):
                picked = []
                for position in range(2):
                    n = inner * per_group + pair * 2 + position
                    slot = step * STEP_GROUPS * per_group + n
                    row = jnp.maximum(rows[side, slot], 0)
                    swapped = (row & 1) ^ position
                    picked.append(table[(side * 2 + swapped) * tiles + row // 2])
                    column = cols[side, slot]
                    column = jnp.where(column >= 0, column & 3, -1)
                    block = weights[side, n]
                    spread.append(
                        jnp.concatenate(
                            [block * as_bf16(lane_col == column), block * as_bf16(lane_col + 2 == column)], axis=1
                        )
                    )
                pieces.append(picked[0] * low_f + picked[1] * high_f)
            product = jnp.dot(
                jnp.concatenate(pieces, axis=1), jnp.concatenate(spread, axis=0), preferred_element_type=jnp.float32
            )
            total = product if total is None else total + product
        out[inner] = total.astype(out.dtype)


def delta_products(rows, cols, sent, weights, groups, width):
    slots = weights.shape[1]
    per_step = slots // groups * STEP_GROUPS
    count = sent[0].shape[1]
    tiles = sum(a.shape[2] for a in sent) // LANES
    return pl.pallas_call(
        delta_kernel,
        grid_spec=pltpu.PrefetchScalarGridSpec(
            num_scalar_prefetch=2,
            grid=(groups // STEP_GROUPS,),
            in_specs=[pl.BlockSpec(a.shape, lambda g, *_: (0, 0, 0)) for a in sent]
            + [pl.BlockSpec((2, per_step, BLK, LANES), lambda g, *_: (0, g, 0, 0))],
            out_specs=pl.BlockSpec((STEP_GROUPS, count, width), lambda g, *_: (g, 0, 0)),
            scratch_shapes=[pltpu.VMEM((4 * tiles, count, LANES), jnp.bfloat16)],
        ),
        out_shape=jax.ShapeDtypeStruct((groups, count, width), jnp.bfloat16),
        compiler_params=pltpu.CompilerParams(vmem_limit_bytes=24 * 2**20),
        cost_estimate=pl.CostEstimate(flops=2 * 10**9, bytes_accessed=20_000_000, transcendentals=0),
    )(rows, cols, *sent, weights)


def base_kernel(tokens, weights, out):
    product = jnp.dot(tokens[...], weights[0], preferred_element_type=jnp.float32)
    out[:, 0, 0] = product.reshape(out.shape[0], out.shape[3], out.shape[4])


def base_products(tokens, weights, planes):
    count, depth = tokens.shape
    columns, _, width = weights.shape
    return pl.pallas_call(
        base_kernel,
        grid=(columns,),
        in_specs=[
            pl.BlockSpec((count, depth), lambda x: (0, 0)),
            pl.BlockSpec((1, depth, width), lambda x: (x, 0, 0)),
        ],
        out_specs=pl.BlockSpec((planes, 1, 1, count // planes, width), lambda x: (0, x // 2, x % 2, 0, 0)),
        out_shape=jax.ShapeDtypeStruct((planes, 2, columns // 2, count // planes, width), jnp.float32),
        compiler_params=pltpu.CompilerParams(vmem_limit_bytes=24 * 2**20),
        cost_estimate=pl.CostEstimate(flops=2 * 10**9, bytes_accessed=8_000_000, transcendentals=0),
    )(tokens, weights)


def place_kernel(core, tokens, rows, out):
    count = out.shape[2]
    token = lax.broadcasted_iota(jnp.int32, (2 * count, 1), 0) + pl.program_id(0) * 2 * count
    hot = as_bf16(tokens[...] == token)
    placed = jnp.dot(hot, rows[...], preferred_element_type=jnp.float32).astype(out.dtype)
    for c in range(2):
        out[c ^ core[0], 0] = placed[c * count : (c + 1) * count]


def place_rows(core, tokens, rows, planes, count):
    width = rows.shape[1]
    return pl.pallas_call(
        place_kernel,
        grid_spec=pltpu.PrefetchScalarGridSpec(
            num_scalar_prefetch=1,
            grid=(planes,),
            in_specs=[
                pl.BlockSpec((1, tokens.shape[1]), lambda z, *_: (0, 0)),
                pl.BlockSpec(rows.shape, lambda z, *_: (0, 0)),
            ],
            out_specs=pl.BlockSpec((2, 1, count, width), lambda z, *_: (0, z, 0, 0)),
        ),
        out_shape=jax.ShapeDtypeStruct((2, planes, count, width), jnp.bfloat16),
        compiler_params=pltpu.CompilerParams(vmem_limit_bytes=24 * 2**20),
        cost_estimate=pl.CostEstimate(flops=2 * 10**9, bytes_accessed=8_000_000, transcendentals=0),
    )(core, tokens, rows)


def core_sum(pair):
    swapped = lax.ppermute(pair[1], "core", CORE_SWAP)
    return (pair[0].astype(jnp.float32) + swapped.astype(jnp.float32)).astype(jnp.bfloat16)


def plane_sum(values):
    parts = lax.all_to_all(values, "z", split_axis=0, concat_axis=0, tiled=True)
    return jnp.sum(parts.astype(jnp.float32), axis=0)


def per_device(hidden, down_weight, delta_blocks, block_rows, block_cols, tenant_ids, tenant_lists):
    core, column, line = lax.axis_index("core"), lax.axis_index("x"), lax.axis_index("y")
    seq_index = lax.axis_index(SEQ)
    plane = lax.axis_index("z")
    seq_count, lines, columns, planes = (lax.axis_size(a) for a in (SEQ, "y", "x", "z"))
    variants, capacity = tenant_lists.shape
    half = capacity // 2
    own_tokens = hidden.shape[0]
    ff_local, width = down_weight.shape
    slots = delta_blocks.shape[1]
    core_ref = core.reshape(1).astype(jnp.int32)

    gathered = lax.all_gather(hidden, "y", axis=0, tiled=True)
    copies = jnp.broadcast_to(down_weight[None], (columns, ff_local, width))
    weights = lax.all_to_all(copies, "x", split_axis=0, concat_axis=0, tiled=True)

    own_blocks = delta_blocks[0].reshape(slots, BLK // 2, 2 * BLK)
    other_blocks = lax.ppermute(own_blocks, "core", CORE_SWAP)
    rows = lax.dynamic_index_in_dim(block_rows, seq_index, 0, False)
    rows = lax.dynamic_slice_in_dim(rows, plane * 2, 2, 0)
    cols = lax.dynamic_index_in_dim(block_cols, seq_index, 0, False)
    cols = lax.dynamic_slice_in_dim(cols, plane * 2, 2, 0)
    lists = lax.dynamic_index_in_dim(tenant_lists.reshape(lines, columns * capacity), line, 0, False)
    token = jnp.arange(lines * own_tokens, dtype=jnp.int32)
    token = ((token // own_tokens) * columns + column) * own_tokens + token % own_tokens
    spread, hot = spread_blocks(
        core_ref, own_blocks, other_blocks, lists[:, None], token[None, :], seq_count
    )

    picked = jnp.dot(hot, gathered, preferred_element_type=jnp.float32).astype(jnp.bfloat16)
    picked = picked.reshape(columns * 2, half, ff_local)
    sent = lax.all_to_all(picked, CHIPS, split_axis=0, concat_axis=0, tiled=True)
    delta = delta_products(rows, cols, [sent], spread, seq_count, width)
    received = lax.all_to_all(delta, SEQ, split_axis=0, concat_axis=0, tiled=True)

    base = base_products(gathered, weights, planes)
    base = lax.psum_scatter(
        base.reshape(planes * 2, columns // 2 * own_tokens, width), TENSOR, scatter_dimension=0, tiled=True
    )
    base = base.reshape(columns // 2, own_tokens, width)
    odd = column % 2
    blocks = []
    for flip in range(2):
        pairs = []
        for x in range(columns):
            for c in range(2):
                pairs.append((x * 2 + c, (2 * c + (x % 2 ^ flip)) * 2 + x // 2))
        mine = lax.dynamic_index_in_dim(base, odd ^ flip, 0, False)
        blocks.append(lax.ppermute(mine, CHIPS, pairs))
    base = jnp.where(odd == 0, jnp.concatenate(blocks, 0), jnp.concatenate(blocks[::-1], 0))

    held = lax.dynamic_index_in_dim(tenant_lists.reshape(variants, 2, half), core, 1, False)
    placed = place_rows(
        core_ref,
        held.reshape(1, variants * half),
        received.reshape(variants * half, width),
        planes,
        base.shape[0],
    )
    return (plane_sum(core_sum(placed)) + base).astype(jnp.bfloat16)


def solution(mesh):
    fine = Mesh(mesh.devices.reshape(8, 4, 8, 2), ("y", "x", "z", "core"))
    return jax.shard_map(
        per_device,
        mesh=fine,
        in_specs=(
            P(SEQ, TENSOR),
            P(TENSOR, SEQ),
            P(SEQ, TENSOR, None),
            P(),
            P(),
            P(),
            P(),
        ),
        out_specs=P(TENSOR, SEQ),
        check_vma=False,
    )
```

time: 225 us -> 182 us (0.81)
  waiting for transfers between devices: 118 us -> 68.6 us
  starting transfers between devices: 20.9 us -> 50.6 us
  blocking collectives: 23.6 us -> 0 us
  matrix products: 10.8 us -> 3.86 us
  local copies, waits for them, and re-layouts: 10.5 us -> 15.4 us
    all_gather x1, waiting for transfers between devices: 95 us -> 11.9 us  [per_device(): gathered = lax.all_gather(hidden, 'y', axis=0, tiled=True)]
    all_to_all x0 -> x3, waiting for transfers between devices: none -> 25 us  [the longest x1 15.8 us: per_device(): lax.all_to_all(picked, CHIPS, split_axis=0, concat_axis=0, tiled=True)]
    all_to_all x0 -> x3, starting transfers between devices: none -> 24 us  [the longest x1 10 us: plane_sum(): parts = lax.all_to_all(values, 'z', split_axis=0, concat_axis=0, tiled=True)]
    all_to_all x1 -> x0, blocking collectives: 23.6 us -> none  [per_device(): parts = lax.all_to_all(summed, 'z', split_axis=0, concat_axis=0, tiled=True)]
    pallas_call x0 -> x2, Pallas kernels: none -> 14.1 us  [the longest x1 8.63 us: spread_blocks(): pl.pallas_call(spread_kernel, grid_spec=pltpu.PrefetchScalarGridSpec(num_...]
    pallas_call x1, Pallas kernels: 20.2 us -> 9.71 us  [delta_products(): pl.pallas_call(delta_kernel, grid_spec=pltpu.PrefetchScalarGridSpec(num_s...]
    dot_general x1 -> x0, matrix products: 6.56 us -> none  [per_device(): base = jnp.dot(gathered, down_weight, preferred_element_type=jnp.float32)]
    ppermute x2 -> x3, starting transfers between devices: 6.63 us -> 12.8 us  [the longest x2 7.9 us: per_device(): blocks.append(lax.ppermute(mine, CHIPS, pairs))]
  transfers between devices with their start and end apart: 5 -> 10, of which waited for: 3 -> 6; matrix products, arithmetic and copies ran while one was open for 7% -> 7% of each run, Pallas kernels for 0% -> 15%
where the time goes in v2:
time: 182 us; the launch traced here: 181 us
  waiting for transfers between devices  68.6 us (38%)
  starting transfers between devices  50.6 us (28%)
  Pallas kernels  27.4 us (15%)
  local copies, waits for them, and re-layouts  15.4 us (8%)
  between operations  13.6 us (7%)
  matrix products  3.86 us (2%)
    all_to_all x1, waiting for transfers between devices, per_device(): lax.all_to_all(delta, SEQ, split_axis=0, concat_axis=0, tiled=True)  25.8 us
    all_to_all x1, waiting for transfers between devices, per_device(): lax.all_to_all(picked, CHIPS, split_axis=0, concat_axis=0, tiled=True)  15.8 us
    all_gather x1, waiting for transfers between devices, per_device(): gathered = lax.all_gather(hidden, 'y', axis=0, tiled=True)  11.9 us
    unnamed x9, local copies, waits for them, and re-layouts  10.2 us
    all_to_all x1, starting transfers between devices, plane_sum(): parts = lax.all_to_all(values, 'z', split_axis=0, concat_axis=0, tiled=True)  10 us
    pallas_call x1, Pallas kernels, delta_products(): pl.pallas_call(delta_kernel, grid_spec=pltpu.PrefetchScalarGridSpec(num_s...  9.71 us
    all_to_all x1, starting transfers between devices, per_device(): lax.all_to_all(picked, CHIPS, split_axis=0, concat_axis=0, tiled=True)  9.16 us
    all_to_all x1, waiting for transfers between devices, plane_sum(): parts = lax.all_to_all(values, 'z', split_axis=0, concat_axis=0, tiled=True)  9.13 us
  transfers between devices with their start and end apart: 10, of which 6 were waited for; matrix products, arithmetic and copies ran while one was open for 7% of the time, Pallas kernels for 15%

profile of v2, /device:TPU:1, one launch (start us, length us, event | category | flops | bytes accessed | tf_op | source)
XLA Modules:
  0.0 181.1 jit_solution(8787712879457715247)
XLA Ops:
  6.5 0.0 all-gather.2.cloned.1.call-start
  6.5 0.7 all-gather.2.cloned.1.call-update
  7.3 3.2 %broadcast_in_dim.5 = bf16[4,1792,256]{2,1,0:T(8,128)(2,1)} broadcast(bf16[1792,256]{1,0:T(8,128)(2,1)} %param.8), dimensions={1,2} | broadcast | bytes 4587520 | tf_op jit(solution)/shard_map/broadcast_in_dim | solution.py:219
  10.5 4.8 %all-to-all-start.3 = ((bf16[4,1792,256]{2,1,0:T(8,128)(2,1)}), bf16[4,1792,256]{2,1,0:T(8,128)(2,1)}, u32[]{:S(2)}, u32[]{:S(2)}) async-start(bf16[4,1792,256]{2,1,0:T(8,128)(2,1)} %broadcast_in_dim.5), calls=%async_computation.3 | async-start | bytes 7340032 | tf_op jit(solution)/shard_map/all_to_all | solution.py:220
  15.3 0.0 copy-start.3
  15.4 2.1 %copy.11 = bf16[32,8,32,128]{3,2,1,0:T(8,128)(2,1)S(1)} copy(bf16[32,8,32,128]{3,1,2,0:T(8,128)(2,1)} %bitcast.33) | data formatting | bytes 4194304
  17.4 8.8 %collective-permute-start = (bf16[256,32,128]{2,1,0:T(8,128)(2,1)S(1)}, bf16[256,32,128]{2,1,0:T(8,128)(2,1)}, u32[]{:S(2)}, u32[]{:S(2)}) collective-permute-start(bf16[256,32,128]{2,1,0:T(8,128)(2,1)S(1)} %bitcast.30), channel_id=1, source_target_pairs={{0,1},{1,0},{2,3},{3,2},{4,5},{5,4},{6,7},{7,6},{8,9},{9,8},{10,11... | collective-permute-start | bytes 6291464 | tf_op jit(solution)/shard_map/ppermute | solution.py:223
  26.2 0.0 copy-done.3
  26.3 0.1 copy.9.lists
  26.5 3.7 %collective-permute-done.other = bf16[256,32,128]{2,1,0:T(8,128)(2,1)} collective-permute-done((bf16[256,32,128]{2,1,0:T(8,128)(2,1)S(1)}, bf16[256,32,128]{2,1,0:T(8,128)(2,1)}, u32[]{:S(2)}, u32[]{:S(2)}) %collective-permute-start) | collective-permute-done | bytes 2097184 | tf_op jit(solution)/shard_map/ppermute | solution.py:223
  30.1 8.6 %shard_map.64 = (bf16[2,256,64,128]{3,2,1,0:T(8,128)(2,1)S(1)}, bf16[512,512]{1,0:T(8,128)(2,1)S(1)}) custom-call(s32[1]{0:T(128)} %bitcast.core, bf16[256,32,128]{2,1,0:T(8,128)(2,1)S(1)} %bitcast.31, bf16[256,32,128]{2,1,0:T(8,128)(2,1)} %collective-permute-done.other, s32[512,1]{1,0:T(8,128)S(1)} %copy.9.lists, s32[1,512]{1,0:T(1,128)S(1)} %fusion.3.tokens), custom_call_target="tpu_custom_call" | custom-call | bytes 40000000 | tf_op jit(solution)/shard_map/pallas_call | solution.py:43
  38.8 0.0 copy-start
  38.8 3.2 %copy-done = bf16[2,256,64,128]{3,2,1,0:T(8,128)(2,1)} copy-done((bf16[2,256,64,128]{3,2,1,0:T(8,128)(2,1)}, bf16[2,256,64,128]{3,2,1,0:T(8,128)(2,1)S(1)}, u32[]{:S(2)}) %copy-start) | copy-done | bytes 8388632
  42.0 11.9 %all-gather.2.cloned.1.call-done.tokens = bf16[512,1792]{1,0:T(8,128)(2,1)} async-done(((bf16[64,1792]{1,0:T(8,128)(2,1)}), bf16[512,1792]{1,0:T(8,128)(2,1)}) %all-gather.2.cloned.1.call-update) | async-done | bytes 1835024 | tf_op jit(solution)/shard_map/all_gather | solution.py:218
  53.9 3.9 %convolution_convert_fusion = bf16[512,1792]{1,0:T(8,128)(2,1)} fusion(bf16[512,512]{1,0:T(8,128)(2,1)S(1)} %get-tuple-element.7, bf16[512,1792]{1,0:T(8,128)(2,1)} %all-gather.2.cloned.1.call-done.tokens), kind=kOutput, calls=%fused_computation | convolution fusion | flops 940441600 | bytes 4194304 | tf_op jit(solution)/shard_map/dot_general | solution.py:235
  57.7 0.0 all-to-all-done.3.weights
  57.7 9.2 %all-to-all-start = ((bf16[8,64,1792]{2,1,0:T(8,128)(2,1)}), bf16[8,64,1792]{2,1,0:T(8,128)(2,1)S(1)}, u32[]{:S(2)}, u32[]{:S(2)}) async-start(bf16[8,64,1792]{2,1,0:T(8,128)(2,1)} %bitcast.34), calls=%async_computation | async-start | bytes 3670016 | tf_op jit(solution)/shard_map/all_to_all | solution.py:237
  66.9 0.0 reduce-scatter.2.cloned.1.call-start
  66.9 0.7 dynamic-slice_bitcast_fusion.3
  67.6 0.0 copy-start.2
  67.7 1.5 copy-done.2
  69.1 5.4 %shard_map.67 = f32[8,2,2,64,256]{4,3,2,1,0:T(8,128)} custom-call(bf16[512,1792]{1,0:T(8,128)(2,1)S(1)} %copy-done.2, bf16[4,1792,256]{2,1,0:T(8,128)(2,1)} %all-to-all-done.3.weights), custom_call_target="tpu_custom_call" | custom-call | flops 2000000000 | bytes 8000000 | tf_op jit(solution)/shard_map/pallas_call | solution.py:154
  74.6 0.0 reduce-scatter.2.cloned.1.call-update
  74.6 15.8 %all-to-all-done.refs_0_ = bf16[8,64,1792]{2,1,0:T(8,128)(2,1)S(1)} async-done(((bf16[8,64,1792]{2,1,0:T(8,128)(2,1)}), bf16[8,64,1792]{2,1,0:T(8,128)(2,1)S(1)}, u32[]{:S(2)}, u32[]{:S(2)}) %all-to-all-start) | async-done | bytes 1835040 | tf_op jit(solution)/shard_map/all_to_all | solution.py:237
  90.4 0.0 copy-start.1
  90.4 3.4 %copy-done.1 = bf16[2,256,64,128]{3,2,1,0:T(8,128)(2,1)S(1)} copy-done((bf16[2,256,64,128]{3,2,1,0:T(8,128)(2,1)S(1)}, bf16[2,256,64,128]{3,2,1,0:T(8,128)(2,1)}, u32[]{:S(2)}) %copy-start.1) | copy-done | bytes 8388632
  93.8 9.7 %shard_map.65 = bf16[32,64,256]{2,1,0:T(8,128)(2,1)} custom-call(s32[2,256]{1,0:T(2,128)S(1)} %get-tuple-element.12.rows, s32[2,256]{1,0:T(2,128)S(1)} %get-tuple-element.11.cols, bf16[8,64,1792]{2,1,0:T(8,128)(2,1)S(1)} %all-to-all-done.refs_0_, bf16[2,256,64,128]{3,2,1,0:T(8,128)(2,1)S(1)} %copy-done.1), custom_call_target="tpu_custom_call" | custom-call | flops 2000000000 | bytes 20000000 | tf_op jit(solution)/shard_map/pallas_call | solution.py:130
  103.5 5.0 %all-to-all-start.1 = ((bf16[32,64,256]{2,1,0:T(8,128)(2,1)}), bf16[32,64,256]{2,1,0:T(8,128)(2,1)S(1)}, u32[]{:S(2)}, u32[]{:S(2)}) async-start(bf16[32,64,256]{2,1,0:T(8,128)(2,1)} %shard_map.65), calls=%async_computation.1 | async-start | bytes 2097152 | tf_op jit(solution)/shard_map/all_to_all | solution.py:239
  108.5 0.1 reshape.93
  108.6 0.1 reshape.94.tokens
  108.7 25.8 %all-to-all-done.1 = bf16[32,64,256]{2,1,0:T(8,128)(2,1)S(1)} async-done(((bf16[32,64,256]{2,1,0:T(8,128)(2,1)}), bf16[32,64,256]{2,1,0:T(8,128)(2,1)S(1)}, u32[]{:S(2)}, u32[]{:S(2)}) %all-to-all-start.1) | async-done | bytes 1048608 | tf_op jit(solution)/shard_map/all_to_all | solution.py:239
  134.5 3.6 %shard_map.66 = bf16[2,8,128,256]{3,2,1,0:T(8,128)(2,1)S(1)} custom-call(s32[1]{0:T(128)} %bitcast.core, s32[1,2048]{1,0:T(1,128)S(1)} %reshape.94.tokens, bf16[2048,256]{1,0:T(8,128)(2,1)S(1)} %bitcast.32), custom_call_target="tpu_custom_call" | custom-call | flops 2000000000 | bytes 8000000 | tf_op jit(solution)/shard_map/pallas_call | solution.py:179
  138.2 4.9 %collective-permute-start.1 = (bf16[8,128,256]{2,1,0:T(8,128)(2,1)S(1)}, bf16[8,128,256]{2,1,0:T(8,128)(2,1)S(1)}, u32[]{:S(2)}, u32[]{:S(2)}) collective-permute-start(bf16[8,128,256]{2,1,0:T(8,128)(2,1)S(1)} %slice_bitcast_fusion), channel_id=1, source_target_pairs={{0,1},{1,0},{2,3},{3,2},{4,5},{5,4},{6,7},{7,6},{8,9},{9,8},{10,11... | collective-permute-start | bytes 1572872 | tf_op jit(solution)/shard_map/ppermute | solution.py:197
  143.1 1.5 collective-permute-done.1
  144.6 0.9 fusion
  145.6 10.0 %all-to-all-start.2 = ((bf16[8,128,256]{2,1,0:T(8,128)(2,1)}), bf16[8,128,256]{2,1,0:T(8,128)(2,1)S(1)}, u32[]{:S(2)}, u32[]{:S(2)}) async-start(bf16[8,128,256]{2,1,0:T(8,128)(2,1)} %fusion), calls=%async_computation.2 | async-start | bytes 1048576 | tf_op jit(solution)/shard_map/all_to_all | solution.py:202
  155.6 0.0 reduce-scatter.2.cloned.1.call-done
  155.6 0.9 dynamic-slice_bitcast_fusion.1
  156.5 5.4 %collective-permute-start.2 = (f32[64,256]{1,0:T(8,128)S(1)}, f32[64,256]{1,0:T(8,128)S(1)}, u32[]{:S(2)}, u32[]{:S(2)}) collective-permute-start(f32[64,256]{1,0:T(8,128)S(1)} %get-tuple-element.9), channel_id=1, source_target_pairs={{0,0},{1,32},{16,16},{17,48},{32,1},{33,33},{48,17},{49,49},{2,2},... | collective-permute-start | bytes 196616 | tf_op jit(solution)/shard_map/ppermute | solution.py:254
  161.9 2.5 %collective-permute-start.3 = (f32[64,256]{1,0:T(8,128)S(1)}, f32[64,256]{1,0:T(8,128)S(1)}, u32[]{:S(2)}, u32[]{:S(2)}) collective-permute-start(f32[64,256]{1,0:T(8,128)S(1)} %get-tuple-element.10), channel_id=1, source_target_pairs={{0,16},{1,48},{16,0},{17,32},{32,17},{33,49},{48,1},{49,33},{2,18}... | collective-permute-start | bytes 196616 | tf_op jit(solution)/shard_map/ppermute | solution.py:254
  164.4 9.1 %all-to-all-done.2 = bf16[8,128,256]{2,1,0:T(8,128)(2,1)S(1)} async-done(((bf16[8,128,256]{2,1,0:T(8,128)(2,1)}), bf16[8,128,256]{2,1,0:T(8,128)(2,1)S(1)}, u32[]{:S(2)}, u32[]{:S(2)}) %all-to-all-start.2) | async-done | bytes 524320 | tf_op jit(solution)/shard_map/all_to_all | solution.py:202
  173.6 0.1 convert_reduce_fusion
  173.6 0.0 collective-permute-done.2
  173.6 0.0 collective-permute-done.3
  173.7 0.7 fusion.2
  (5 shorter events, 0.1 us)
Async XLA Ops:
  6.5 47.3 %all-gather.2.cloned.1.call-start = ((), (), s32[]{:S(2)}) async-start(), calls=%async_computation.5 | async-start | bytes 2064384 | tf_op jit(solution)/shard_map/all_gather | solution.py:218
  10.5 47.2 %all-to-all-start.3 = ((bf16[4,1792,256]{2,1,0:T(8,128)(2,1)}), bf16[4,1792,256]{2,1,0:T(8,128)(2,1)}, u32[]{:S(2)}, u32[]{:S(2)}) async-start(bf16[4,1792,256]{2,1,0:T(8,128)(2,1)} %broadcast_in_dim.5), calls=%async_computation.3 | async-start | bytes 7340032 | tf_op jit(solution)/shard_map/all_to_all | solution.py:220
  15.3 10.9 %copy-start.3 = (s32[32,128]{1,0:T(8,128)S(1)}, s32[32,128]{1,0:T(8,128)}, u32[]{:S(2)}) copy-start(s32[32,128]{1,0:T(8,128)} %param.12) | copy-start | bytes 49156
  17.4 12.7 %collective-permute-start = (bf16[256,32,128]{2,1,0:T(8,128)(2,1)S(1)}, bf16[256,32,128]{2,1,0:T(8,128)(2,1)}, u32[]{:S(2)}, u32[]{:S(2)}) collective-permute-start(bf16[256,32,128]{2,1,0:T(8,128)(2,1)S(1)} %bitcast.30), channel_id=1, source_target_pairs={{0,1},{1,0},{2,3},{3,2},{4,5},{5,4},{6,7},{7,6},{8,9},{9,8},{10,11... | collective-permute-start | bytes 6291464 | tf_op jit(solution)/shard_map/ppermute | solution.py:223
  38.8 3.2 %copy-start = (bf16[2,256,64,128]{3,2,1,0:T(8,128)(2,1)}, bf16[2,256,64,128]{3,2,1,0:T(8,128)(2,1)S(1)}, u32[]{:S(2)}) copy-start(bf16[2,256,64,128]{3,2,1,0:T(8,128)(2,1)S(1)} %get-tuple-element.8.refs_1_) | copy-start | bytes 25165828
  57.7 32.7 %all-to-all-start = ((bf16[8,64,1792]{2,1,0:T(8,128)(2,1)}), bf16[8,64,1792]{2,1,0:T(8,128)(2,1)S(1)}, u32[]{:S(2)}, u32[]{:S(2)}) async-start(bf16[8,64,1792]{2,1,0:T(8,128)(2,1)} %bitcast.34), calls=%async_computation | async-start | bytes 3670016 | tf_op jit(solution)/shard_map/all_to_all | solution.py:237
  66.9 88.7 %reduce-scatter.2.cloned.1.call-start = ((), (), s32[]{:S(2)}) async-start(), calls=%async_computation.6 | async-start | bytes 2228224 | tf_op jit(solution)/shard_map/reduce_scatter | solution.py:242
  67.6 1.5 copy-start.2
  90.4 3.4 %copy-start.1 = (bf16[2,256,64,128]{3,2,1,0:T(8,128)(2,1)S(1)}, bf16[2,256,64,128]{3,2,1,0:T(8,128)(2,1)}, u32[]{:S(2)}) copy-start(bf16[2,256,64,128]{3,2,1,0:T(8,128)(2,1)} %copy-done) | copy-start | bytes 25165828
  103.5 31.0 %all-to-all-start.1 = ((bf16[32,64,256]{2,1,0:T(8,128)(2,1)}), bf16[32,64,256]{2,1,0:T(8,128)(2,1)S(1)}, u32[]{:S(2)}, u32[]{:S(2)}) async-start(bf16[32,64,256]{2,1,0:T(8,128)(2,1)} %shard_map.65), calls=%async_computation.1 | async-start | bytes 2097152 | tf_op jit(solution)/shard_map/all_to_all | solution.py:239
  138.2 6.4 %collective-permute-start.1 = (bf16[8,128,256]{2,1,0:T(8,128)(2,1)S(1)}, bf16[8,128,256]{2,1,0:T(8,128)(2,1)S(1)}, u32[]{:S(2)}, u32[]{:S(2)}) collective-permute-start(bf16[8,128,256]{2,1,0:T(8,128)(2,1)S(1)} %slice_bitcast_fusion), channel_id=1, source_target_pairs={{0,1},{1,0},{2,3},{3,2},{4,5},{5,4},{6,7},{7,6},{8,9},{9,8},{10,11... | collective-permute-start | bytes 1572872 | tf_op jit(solution)/shard_map/ppermute | solution.py:197
  145.6 28.0 %all-to-all-start.2 = ((bf16[8,128,256]{2,1,0:T(8,128)(2,1)}), bf16[8,128,256]{2,1,0:T(8,128)(2,1)S(1)}, u32[]{:S(2)}, u32[]{:S(2)}) async-start(bf16[8,128,256]{2,1,0:T(8,128)(2,1)} %fusion), calls=%async_computation.2 | async-start | bytes 1048576 | tf_op jit(solution)/shard_map/all_to_all | solution.py:202
  156.5 17.1 %collective-permute-start.2 = (f32[64,256]{1,0:T(8,128)S(1)}, f32[64,256]{1,0:T(8,128)S(1)}, u32[]{:S(2)}, u32[]{:S(2)}) collective-permute-start(f32[64,256]{1,0:T(8,128)S(1)} %get-tuple-element.9), channel_id=1, source_target_pairs={{0,0},{1,32},{16,16},{17,48},{32,1},{33,33},{48,17},{49,49},{2,2},... | collective-permute-start | bytes 196616 | tf_op jit(solution)/shard_map/ppermute | solution.py:254
  161.9 11.8 %collective-permute-start.3 = (f32[64,256]{1,0:T(8,128)S(1)}, f32[64,256]{1,0:T(8,128)S(1)}, u32[]{:S(2)}, u32[]{:S(2)}) collective-permute-start(f32[64,256]{1,0:T(8,128)S(1)} %get-tuple-element.10), channel_id=1, source_target_pairs={{0,16},{1,48},{16,0},{17,32},{32,17},{33,49},{48,1},{49,33},{2,18}... | collective-permute-start | bytes 196616 | tf_op jit(solution)/shard_map/ppermute | solution.py:254
Sparse Core Ops, SparseCore 0:
  9.4 44.3 all-gather.1
  74.7 62.0 reduce-scatter.1

commit v3 on v2

--- a/solution.py
+++ b/solution.py
@@ -11,7 +11,7 @@
 TENSOR = ("z", "core")
 CHIPS = ("x", "core")
 CORE_SWAP = [(0, 1), (1, 0)]
-STEP_GROUPS = 2
+STEP_GROUPS = 4
 SPREAD_GROUPS = 4
 
 
@@ -60,15 +60,25 @@
             jax.ShapeDtypeStruct((2, slots, BLK, LANES), jnp.bfloat16),
             jax.ShapeDtypeStruct((picks, tokens.shape[1]), jnp.bfloat16),
         ],
-        compiler_params=pltpu.CompilerParams(vmem_limit_bytes=16 * 2**20),
+        compiler_params=pltpu.CompilerParams(vmem_limit_bytes=56 * 2**20),
         cost_estimate=pl.CostEstimate(flops=0, bytes_accessed=40_000_000, transcendentals=0),
     )(core, own, other, lists, tokens)
 
 
 def delta_kernel(rows, cols, *refs):
-    *sent, weights, out, table = refs
-    step = pl.program_id(0)
-    per_group = weights.shape[1] // STEP_GROUPS
+    *sent, stored, out, table, weights, arrived = refs
+    step, steps = pl.program_id(0), arrived.shape[0]
+    count = stored.shape[1] // steps
+    per_group = count // STEP_GROUPS
+
+    def fetch(at):
+        slots = pl.ds(pl.multiple_of(at * count, count), count)
+        return pltpu.make_async_copy(stored.at[:, slots], weights.at[:, slots], arrived.at[at])
+
+    @pl.when(step == 0)
+    def _():
+        lax.fori_loop(0, steps, lambda at, _: fetch(at).start(), None)
+
     tiles = sum(ref.shape[2] for ref in sent) // LANES
     lane_col = lax.broadcasted_iota(jnp.int32, (1, LANES), 1) // BLK
     low_f, high_f = as_bf16(lane_col == 0), as_bf16(lane_col == 1)
@@ -94,6 +104,7 @@
                     table[(side * 2 + 1) * tiles + tile] = both[:, LANES:]
                     tile += 1
 
+    fetch(step).wait()
     for inner in range(STEP_GROUPS):
         total = None
         for side in range(2):
@@ -108,7 +119,7 @@
                     picked.append(table[(side * 2 + swapped) * tiles + row // 2])
                     column = cols[side, slot]
                     column = jnp.where(column >= 0, column & 3, -1)
-                    block = weights[side, n]
+                    block = weights[side, step * count + n]
                     spread.append(
                         jnp.concatenate(
                             [block * as_bf16(lane_col == column), block * as_bf16(lane_col + 2 == column)], axis=1
@@ -123,8 +134,6 @@
 
 
 def delta_products(rows, cols, sent, weights, groups, width):
-    slots = weights.shape[1]
-    per_step = slots // groups * STEP_GROUPS
     count = sent[0].shape[1]
     tiles = sum(a.shape[2] for a in sent) // LANES
     return pl.pallas_call(
@@ -133,14 +142,43 @@
             num_scalar_prefetch=2,
             grid=(groups // STEP_GROUPS,),
             in_specs=[pl.BlockSpec(a.shape, lambda g, *_: (0, 0, 0)) for a in sent]
-            + [pl.BlockSpec((2, per_step, BLK, LANES), lambda g, *_: (0, g, 0, 0))],
+            + [pl.BlockSpec(memory_space=pl.ANY)],
             out_specs=pl.BlockSpec((STEP_GROUPS, count, width), lambda g, *_: (g, 0, 0)),
-            scratch_shapes=[pltpu.VMEM((4 * tiles, count, LANES), jnp.bfloat16)],
+            scratch_shapes=[
+                pltpu.VMEM((4 * tiles, count, LANES), jnp.bfloat16),
+                pltpu.VMEM(weights.shape, jnp.bfloat16),
+                pltpu.SemaphoreType.DMA((groups // STEP_GROUPS,)),
+            ],
         ),
         out_shape=jax.ShapeDtypeStruct((groups, count, width), jnp.bfloat16),
-        compiler_params=pltpu.CompilerParams(vmem_limit_bytes=24 * 2**20),
+        compiler_params=pltpu.CompilerParams(vmem_limit_bytes=48 * 2**20),
         cost_estimate=pl.CostEstimate(flops=2 * 10**9, bytes_accessed=20_000_000, transcendentals=0),
     )(rows, cols, *sent, weights)
+
+
+def pick_kernel(hot, *refs):
+    *parts, out = refs
+    at = 0
+    for part in parts:
+        depth = part.shape[1]
+        picked = jnp.dot(hot[...], part[...], preferred_element_type=jnp.float32)
+        out[:, at : at + depth] = picked.astype(out.dtype)
+        at += depth
+
+
+def pick_rows(hot, parts):
+    picks, count = hot.shape
+    depth = sum(a.shape[1] for a in parts)
+    return pl.pallas_call(
+        pick_kernel,
+        grid=(2,),
+        in_specs=[pl.BlockSpec((picks // 2, count), lambda g: (g, 0))]
+        + [pl.BlockSpec(a.shape, lambda g: (0, 0)) for a in parts],
+        out_specs=pl.BlockSpec((picks // 2, depth), lambda g: (g, 0)),
+        out_shape=jax.ShapeDtypeStruct((picks, depth), jnp.bfloat16),
+        compiler_params=pltpu.CompilerParams(vmem_limit_bytes=56 * 2**20),
+        cost_estimate=pl.CostEstimate(flops=10**9, bytes_accessed=4_000_000, transcendentals=0),
+    )(hot, *parts)
 
 
 def base_kernel(tokens, weights, out):
@@ -165,37 +203,37 @@
     )(tokens, weights)
 
 
-def place_kernel(core, tokens, rows, out):
-    count = out.shape[2]
-    token = lax.broadcasted_iota(jnp.int32, (2 * count, 1), 0) + pl.program_id(0) * 2 * count
-    hot = as_bf16(tokens[...] == token)
-    placed = jnp.dot(hot, rows[...], preferred_element_type=jnp.float32).astype(out.dtype)
-    for c in range(2):
-        out[c ^ core[0], 0] = placed[c * count : (c + 1) * count]
-
-
-def place_rows(core, tokens, rows, planes, count):
+def place_kernel(core, lists, rows, *refs):
+    *before, out = refs
+    planes, count, width = out.shape
+    at = lax.broadcasted_iota(jnp.int32, (planes * count, 1), 0) + pl.program_id(0) * planes * count
+    token = (at // count * 2 + core[0]) * count + at % count
+    hot = as_bf16(lists[...] == token)
+    placed = jnp.dot(hot, rows[...], preferred_element_type=jnp.float32).reshape(out.shape)
+    if before:
+        placed = placed + before[0][...]
+    out[...] = placed.astype(out.dtype)
+
+
+def place_rows(core, lists, rows, planes, count, *before):
     width = rows.shape[1]
+    block = pl.BlockSpec((2, count, width), lambda z, *_: (z, 0, 0))
     return pl.pallas_call(
         place_kernel,
         grid_spec=pltpu.PrefetchScalarGridSpec(
             num_scalar_prefetch=1,
-            grid=(planes,),
+            grid=(planes // 2,),
             in_specs=[
-                pl.BlockSpec((1, tokens.shape[1]), lambda z, *_: (0, 0)),
+                pl.BlockSpec((1, lists.shape[1]), lambda z, *_: (0, 0)),
                 pl.BlockSpec(rows.shape, lambda z, *_: (0, 0)),
-            ],
-            out_specs=pl.BlockSpec((2, 1, count, width), lambda z, *_: (0, z, 0, 0)),
+            ]
+            + [block] * len(before),
+            out_specs=block,
         ),
-        out_shape=jax.ShapeDtypeStruct((2, planes, count, width), jnp.bfloat16),
+        out_shape=jax.ShapeDtypeStruct((planes, count, width), jnp.bfloat16),
         compiler_params=pltpu.CompilerParams(vmem_limit_bytes=24 * 2**20),
-        cost_estimate=pl.CostEstimate(flops=2 * 10**9, bytes_accessed=8_000_000, transcendentals=0),
-    )(core, tokens, rows)
-
-
-def core_sum(pair):
-    swapped = lax.ppermute(pair[1], "core", CORE_SWAP)
-    return (pair[0].astype(jnp.float32) + swapped.astype(jnp.float32)).astype(jnp.bfloat16)
+        cost_estimate=pl.CostEstimate(flops=10**9, bytes_accessed=4_000_000, transcendentals=0),
+    )(core, lists, rows, *before)
 
 
 def plane_sum(values):
@@ -232,9 +270,8 @@
         core_ref, own_blocks, other_blocks, lists[:, None], token[None, :], seq_count
     )
 
-    picked = jnp.dot(hot, gathered, preferred_element_type=jnp.float32).astype(jnp.bfloat16)
-    picked = picked.reshape(columns * 2, half, ff_local)
-    sent = lax.all_to_all(picked, CHIPS, split_axis=0, concat_axis=0, tiled=True)
+    picked = pick_rows(hot, (gathered,))
+    sent = lax.all_to_all(picked.reshape(columns * 2, half, ff_local), CHIPS, split_axis=0, concat_axis=0, tiled=True)
     delta = delta_products(rows, cols, [sent], spread, seq_count, width)
     received = lax.all_to_all(delta, SEQ, split_axis=0, concat_axis=0, tiled=True)
 
@@ -254,15 +291,14 @@
         blocks.append(lax.ppermute(mine, CHIPS, pairs))
     base = jnp.where(odd == 0, jnp.concatenate(blocks, 0), jnp.concatenate(blocks[::-1], 0))
 
-    held = lax.dynamic_index_in_dim(tenant_lists.reshape(variants, 2, half), core, 1, False)
-    placed = place_rows(
-        core_ref,
-        held.reshape(1, variants * half),
-        received.reshape(variants * half, width),
-        planes,
-        base.shape[0],
-    )
-    return (plane_sum(core_sum(placed)) + base).astype(jnp.bfloat16)
+    lists = tenant_lists.reshape(variants, 2, half)
+    received = received.reshape(variants * half, width)
+    swapped = lax.ppermute(received, "core", CORE_SWAP)
+    placed = ()
+    for side, moved in ((core, received), (1 - core, swapped)):
+        held = lax.dynamic_index_in_dim(lists, side, 1, False).reshape(1, variants * half)
+        placed = (place_rows(core_ref, held, moved, planes, base.shape[0], *placed),)
+    return (plane_sum(placed[0]) + base).astype(jnp.bfloat16)
 
 
 def solution(mesh):

time: 182 us -> 175 us (0.962)
  blocking collectives: 0 us -> 30.8 us
  waiting for transfers between devices: 68.6 us -> 38.4 us
  Pallas kernels: 27.4 us -> 34.2 us
  local copies, waits for them, and re-layouts: 15.4 us -> 9.64 us
  starting transfers between devices: 50.6 us -> 45.5 us
  matrix products: 3.86 us -> 0 us
    all_to_all x0 -> x1, blocking collectives: none -> 30.8 us  [per_device(): lax.all_to_all(delta, SEQ, split_axis=0, concat_axis=0, tiled=True)]
    all_to_all x2 -> x1, waiting for transfers between devices: 41.6 us -> 15.8 us  [per_device(): lax.all_to_all(picked.reshape(columns * 2, half, ff_local), CHIPS, split_...]
    unnamed x9 -> x7, local copies, waits for them, and re-layouts: 10.2 us -> 3.58 us
    all_to_all x2 -> x1, starting transfers between devices: 14.1 us -> 9.2 us  [per_device(): lax.all_to_all(picked.reshape(columns * 2, half, ff_local), CHIPS, split_...]
    pallas_call x1, Pallas kernels: 8.63 us -> 13.3 us  [spread_blocks(): pl.pallas_call(spread_kernel, grid_spec=pltpu.PrefetchScalarGridSpec(num_...]
    dot_general x1 -> x0, matrix products: 3.86 us -> none  [per_device(): jnp.dot(hot, gathered, preferred_element_type=jnp.float32)]
    pallas_call x0 -> x1, Pallas kernels: none -> 3.84 us  [pick_rows(): pl.pallas_call(pick_kernel, grid=(2,), in_specs=[pl.BlockSpec((picks // 2...]
    pallas_call x1, Pallas kernels: 9.71 us -> 6.84 us  [delta_products(): pl.pallas_call(delta_kernel, grid_spec=pltpu.PrefetchScalarGridSpec(num_s...]
  transfers between devices with their start and end apart: 10 -> 9, of which waited for: 6 -> 4; matrix products, arithmetic and copies ran while one was open for 7% -> 5% of each run, Pallas kernels for 15% -> 20%
where the time goes in v3:
time: 175 us; the launch traced here: 173 us
  starting transfers between devices  45.5 us (26%)
  waiting for transfers between devices  38.4 us (22%)
  Pallas kernels  34.2 us (20%)
  blocking collectives  30.8 us (18%)
  between operations  13.6 us (8%)
  local copies, waits for them, and re-layouts  9.64 us (6%)
    all_to_all x1, blocking collectives, per_device(): lax.all_to_all(delta, SEQ, split_axis=0, concat_axis=0, tiled=True)  30.8 us
    all_to_all x1, waiting for transfers between devices, per_device(): lax.all_to_all(picked.reshape(columns * 2, half, ff_local), CHIPS, split_...  15.8 us
    pallas_call x1, Pallas kernels, spread_blocks(): pl.pallas_call(spread_kernel, grid_spec=pltpu.PrefetchScalarGridSpec(num_...  13.3 us
    all_gather x1, waiting for transfers between devices, per_device(): gathered = lax.all_gather(hidden, 'y', axis=0, tiled=True)  10.4 us
    all_to_all x1, starting transfers between devices, plane_sum(): parts = lax.all_to_all(values, 'z', split_axis=0, concat_axis=0, tiled=True)  9.78 us
    all_to_all x1, starting transfers between devices, per_device(): lax.all_to_all(picked.reshape(columns * 2, half, ff_local), CHIPS, split_...  9.2 us
    all_to_all x1, waiting for transfers between devices, plane_sum(): parts = lax.all_to_all(values, 'z', split_axis=0, concat_axis=0, tiled=True)  9.01 us
    ppermute x1, starting transfers between devices, per_device(): other_blocks = lax.ppermute(own_blocks, 'core', CORE_SWAP)  8.78 us
  transfers between devices with their start and end apart: 9, of which 4 were waited for; matrix products, arithmetic and copies ran while one was open for 5% of the time, Pallas kernels for 20%

profile of v3, /device:TPU:1, one launch (start us, length us, event | category | flops | bytes accessed | tf_op | source)
XLA Modules:
  0.0 173.4 jit_solution(10192393931175034373)
XLA Ops:
  6.5 0.0 all-gather.2.cloned.1.call-start
  6.5 0.7 all-gather.2.cloned.1.call-update
  7.3 3.3 %broadcast_in_dim.5 = bf16[4,1792,256]{2,1,0:T(8,128)(2,1)} broadcast(bf16[1792,256]{1,0:T(8,128)(2,1)} %param.8), dimensions={1,2} | broadcast | bytes 4587520 | tf_op jit(solution)/shard_map/broadcast_in_dim | solution.py:257
  10.5 4.8 %all-to-all-start.3 = ((bf16[4,1792,256]{2,1,0:T(8,128)(2,1)}), bf16[4,1792,256]{2,1,0:T(8,128)(2,1)}, u32[]{:S(2)}, u32[]{:S(2)}) async-start(bf16[4,1792,256]{2,1,0:T(8,128)(2,1)} %broadcast_in_dim.5), calls=%async_computation.3 | async-start | bytes 7340032 | tf_op jit(solution)/shard_map/all_to_all | solution.py:258
  15.3 0.0 copy-start.2
  15.4 2.1 %copy.14 = bf16[32,8,32,128]{3,2,1,0:T(8,128)(2,1)S(1)} copy(bf16[32,8,32,128]{3,1,2,0:T(8,128)(2,1)} %bitcast.29) | data formatting | bytes 4194304
  17.4 0.0 copy-start.1
  17.4 8.8 %collective-permute-start = (bf16[256,32,128]{2,1,0:T(8,128)(2,1)S(1)}, bf16[256,32,128]{2,1,0:T(8,128)(2,1)}, u32[]{:S(2)}, u32[]{:S(2)}) collective-permute-start(bf16[256,32,128]{2,1,0:T(8,128)(2,1)S(1)} %bitcast.26), channel_id=1, source_target_pairs={{0,1},{1,0},{2,3},{3,2},{4,5},{5,4},{6,7},{7,6},{8,9},{9,8},{10,11... | collective-permute-start | bytes 6291464 | tf_op jit(solution)/shard_map/ppermute | solution.py:261
  26.2 0.0 copy-done.2
  26.3 0.9 copy.10.lists
  27.2 0.6 fusion.2.tokens
  27.8 2.4 %collective-permute-done.other = bf16[256,32,128]{2,1,0:T(8,128)(2,1)} collective-permute-done((bf16[256,32,128]{2,1,0:T(8,128)(2,1)S(1)}, bf16[256,32,128]{2,1,0:T(8,128)(2,1)}, u32[]{:S(2)}, u32[]{:S(2)}) %collective-permute-start) | collective-permute-done | bytes 2097184 | tf_op jit(solution)/shard_map/ppermute | solution.py:261
  30.1 0.0 copy-done.1
  30.1 13.3 %shard_map.64 = (bf16[2,256,64,128]{3,2,1,0:T(8,128)(2,1)}, bf16[512,512]{1,0:T(8,128)(2,1)}) custom-call(s32[1]{0:T(128)} %bitcast.core, bf16[256,32,128]{2,1,0:T(8,128)(2,1)} %bitcast.27, bf16[256,32,128]{2,1,0:T(8,128)(2,1)} %collective-permute-done.other, s32[512,1]{1,0:T(8,128)} %copy.10.lists, s32[1,512]{1,0:T(1,128)} %fusion.2.tokens), custom_call_target="tpu_custom_call" | custom-call | bytes 40000000 | tf_op jit(solution)/shard_map/pallas_call | solution.py:43
  43.4 10.4 %all-gather.2.cloned.1.call-done.refs_0_.tokens = bf16[512,1792]{1,0:T(8,128)(2,1)} async-done(((bf16[64,1792]{1,0:T(8,128)(2,1)}), bf16[512,1792]{1,0:T(8,128)(2,1)}) %all-gather.2.cloned.1.call-update) | async-done | bytes 1835024 | tf_op jit(solution)/shard_map/all_gather | solution.py:256
  53.9 3.8 %shard_map.65 = bf16[512,1792]{1,0:T(8,128)(2,1)} custom-call(bf16[512,512]{1,0:T(8,128)(2,1)} %get-tuple-element.7.hot, bf16[512,1792]{1,0:T(8,128)(2,1)} %all-gather.2.cloned.1.call-done.refs_0_.tokens), custom_call_target="tpu_custom_call" | custom-call | flops 1000000000 | bytes 4000000 | tf_op jit(solution)/shard_map/pallas_call | solution.py:172
  57.7 0.0 all-to-all-done.3.weights
  57.7 9.2 %all-to-all-start = ((bf16[8,64,1792]{2,1,0:T(8,128)(2,1)}), bf16[8,64,1792]{2,1,0:T(8,128)(2,1)S(1)}, u32[]{:S(2)}, u32[]{:S(2)}) async-start(bf16[8,64,1792]{2,1,0:T(8,128)(2,1)} %bitcast.28), calls=%async_computation | async-start | bytes 3670016 | tf_op jit(solution)/shard_map/all_to_all | solution.py:274
  66.9 0.0 reduce-scatter.2.cloned.1.call-start
  66.9 0.0 copy-start
  66.9 1.5 copy-done
  68.4 5.4 %shard_map.69 = f32[8,2,2,64,256]{4,3,2,1,0:T(8,128)} custom-call(bf16[512,1792]{1,0:T(8,128)(2,1)S(1)} %copy-done, bf16[4,1792,256]{2,1,0:T(8,128)(2,1)} %all-to-all-done.3.weights), custom_call_target="tpu_custom_call" | custom-call | flops 2000000000 | bytes 8000000 | tf_op jit(solution)/shard_map/pallas_call | solution.py:192
  73.8 0.0 reduce-scatter.2.cloned.1.call-update
  73.9 0.8 dynamic-slice_bitcast_fusion.3
  74.6 15.8 %all-to-all-done.refs_0_ = bf16[8,64,1792]{2,1,0:T(8,128)(2,1)S(1)} async-done(((bf16[8,64,1792]{2,1,0:T(8,128)(2,1)}), bf16[8,64,1792]{2,1,0:T(8,128)(2,1)S(1)}, u32[]{:S(2)}, u32[]{:S(2)}) %all-to-all-start) | async-done | bytes 1835040 | tf_op jit(solution)/shard_map/all_to_all | solution.py:274
  90.4 6.8 %shard_map.66 = bf16[32,64,256]{2,1,0:T(8,128)(2,1)S(1)} custom-call(s32[2,256]{1,0:T(2,128)S(1)} %get-tuple-element.14.rows, s32[2,256]{1,0:T(2,128)S(1)} %get-tuple-element.13.cols, bf16[8,64,1792]{2,1,0:T(8,128)(2,1)S(1)} %all-to-all-done.refs_0_, bf16[2,256,64,128]{3,2,1,0:T(8,128)(2,1)} %get-tuple-element.8.refs_1_), custom_call_target="tpu_custom_call" | custom-call | flops 2000000000 | bytes 20000000 | tf_op jit(solution)/shard_map/pallas_call | solution.py:139
  97.3 30.8 %all_to_all.20 = bf16[32,64,256]{2,1,0:T(8,128)(2,1)S(1)} all-to-all(bf16[32,64,256]{2,1,0:T(8,128)(2,1)S(1)} %shard_map.66), channel_id=1, replica_groups=mesh['y'=8,'x'=4,'z'=8,'core'=2] {'y','x'}, dimensions={0} | all-to-all | bytes 2097152 | tf_op jit(solution)/shard_map/all_to_all | solution.py:276
  128.1 4.9 %collective-permute-start.1 = (bf16[2048,256]{1,0:T(8,128)(2,1)S(1)}, bf16[2048,256]{1,0:T(8,128)(2,1)S(1)}, u32[]{:S(2)}, u32[]{:S(2)}) collective-permute-start(bf16[2048,256]{1,0:T(8,128)(2,1)S(1)} %bitcast.24), channel_id=1, source_target_pairs={{0,1},{1,0},{2,3},{3,2},{4,5},{5,4},{6,7},{7,6},{8,9},{9,8},{10,11... | collective-permute-start | bytes 3145736 | tf_op jit(solution)/shard_map/ppermute | solution.py:296
  133.0 0.1 reshape.95
  133.2 0.1 reshape.100.lists
  133.2 0.1 reshape.96.lists
  133.3 2.0 %shard_map.67.refs_0_ = bf16[8,128,256]{2,1,0:T(8,128)(2,1)S(1)} custom-call(s32[1]{0:T(128)} %bitcast.core, s32[1,2048]{1,0:T(1,128)S(1)} %reshape.100.lists, bf16[2048,256]{1,0:T(8,128)(2,1)S(1)} %bitcast.25), custom_call_target="tpu_custom_call" | custom-call | flops 1000000000 | bytes 4000000 | tf_op jit(solution)/shard_map/pallas_call | solution.py:221
  135.3 0.0 collective-permute-done.1.rows
  135.3 2.8 %shard_map.68 = bf16[8,128,256]{2,1,0:T(8,128)(2,1)} custom-call(s32[1]{0:T(128)} %bitcast.core, s32[1,2048]{1,0:T(1,128)S(1)} %reshape.96.lists, bf16[2048,256]{1,0:T(8,128)(2,1)S(1)} %collective-permute-done.1.rows, bf16[8,128,256]{2,1,0:T(8,128)(2,1)S(1)} %shard_map.67.refs_0_), custom_call_target="tpu_custom_call" | custom-call | flops 1000000000 | bytes 4000000 | tf_op jit(solution)/shard_map/pallas_call | solution.py:221
  138.1 9.8 %all-to-all-start.2 = ((bf16[8,128,256]{2,1,0:T(8,128)(2,1)}), bf16[8,128,256]{2,1,0:T(8,128)(2,1)S(1)}, u32[]{:S(2)}, u32[]{:S(2)}) async-start(bf16[8,128,256]{2,1,0:T(8,128)(2,1)} %shard_map.68), calls=%async_computation.2 | async-start | bytes 1048576 | tf_op jit(solution)/shard_map/all_to_all | solution.py:240
  147.9 0.0 reduce-scatter.2.cloned.1.call-done
  147.9 0.9 dynamic-slice_bitcast_fusion.1
  148.8 5.4 %collective-permute-start.2 = (f32[64,256]{1,0:T(8,128)S(1)}, f32[64,256]{1,0:T(8,128)S(1)}, u32[]{:S(2)}, u32[]{:S(2)}) collective-permute-start(f32[64,256]{1,0:T(8,128)S(1)} %get-tuple-element.9), channel_id=1, source_target_pairs={{0,0},{1,32},{16,16},{17,48},{32,1},{33,33},{48,17},{49,49},{2,2},... | collective-permute-start | bytes 196616 | tf_op jit(solution)/shard_map/ppermute | solution.py:291
  154.2 2.6 %collective-permute-start.3 = (f32[64,256]{1,0:T(8,128)S(1)}, f32[64,256]{1,0:T(8,128)S(1)}, u32[]{:S(2)}, u32[]{:S(2)}) collective-permute-start(f32[64,256]{1,0:T(8,128)S(1)} %get-tuple-element.10), channel_id=1, source_target_pairs={{0,16},{1,48},{16,0},{17,32},{32,17},{33,49},{48,1},{49,33},{2,18}... | collective-permute-start | bytes 196616 | tf_op jit(solution)/shard_map/ppermute | solution.py:291
  156.8 9.0 %all-to-all-done.2 = bf16[8,128,256]{2,1,0:T(8,128)(2,1)S(1)} async-done(((bf16[8,128,256]{2,1,0:T(8,128)(2,1)}), bf16[8,128,256]{2,1,0:T(8,128)(2,1)S(1)}, u32[]{:S(2)}, u32[]{:S(2)}) %all-to-all-start.2) | async-done | bytes 524320 | tf_op jit(solution)/shard_map/all_to_all | solution.py:240
  165.8 0.1 convert_reduce_fusion
  165.9 0.0 collective-permute-done.2
  165.9 0.0 collective-permute-done.3
  165.9 0.7 fusion.1
  (3 shorter events, 0.1 us)
Async XLA Ops:
  6.5 47.3 %all-gather.2.cloned.1.call-start = ((), (), s32[]{:S(2)}) async-start(), calls=%async_computation.5 | async-start | bytes 2064384 | tf_op jit(solution)/shard_map/all_gather | solution.py:256
  10.5 47.2 %all-to-all-start.3 = ((bf16[4,1792,256]{2,1,0:T(8,128)(2,1)}), bf16[4,1792,256]{2,1,0:T(8,128)(2,1)}, u32[]{:S(2)}, u32[]{:S(2)}) async-start(bf16[4,1792,256]{2,1,0:T(8,128)(2,1)} %broadcast_in_dim.5), calls=%async_computation.3 | async-start | bytes 7340032 | tf_op jit(solution)/shard_map/all_to_all | solution.py:258
  15.3 10.9 %copy-start.2 = (s32[32,128]{1,0:T(8,128)S(1)}, s32[32,128]{1,0:T(8,128)}, u32[]{:S(2)}) copy-start(s32[32,128]{1,0:T(8,128)} %param.12) | copy-start | bytes 49156
  17.4 12.7 %copy-start.1 = (bf16[32,8,32,128]{3,2,1,0:T(8,128)(2,1)}, bf16[32,8,32,128]{3,2,1,0:T(8,128)(2,1)S(1)}, u32[]{:S(2)}) copy-start(bf16[32,8,32,128]{3,2,1,0:T(8,128)(2,1)S(1)} %copy.14) | copy-start | bytes 6291460
  17.4 12.7 %collective-permute-start = (bf16[256,32,128]{2,1,0:T(8,128)(2,1)S(1)}, bf16[256,32,128]{2,1,0:T(8,128)(2,1)}, u32[]{:S(2)}, u32[]{:S(2)}) collective-permute-start(bf16[256,32,128]{2,1,0:T(8,128)(2,1)S(1)} %bitcast.26), channel_id=1, source_target_pairs={{0,1},{1,0},{2,3},{3,2},{4,5},{5,4},{6,7},{7,6},{8,9},{9,8},{10,11... | collective-permute-start | bytes 6291464 | tf_op jit(solution)/shard_map/ppermute | solution.py:261
  57.7 32.7 %all-to-all-start = ((bf16[8,64,1792]{2,1,0:T(8,128)(2,1)}), bf16[8,64,1792]{2,1,0:T(8,128)(2,1)S(1)}, u32[]{:S(2)}, u32[]{:S(2)}) async-start(bf16[8,64,1792]{2,1,0:T(8,128)(2,1)} %bitcast.28), calls=%async_computation | async-start | bytes 3670016 | tf_op jit(solution)/shard_map/all_to_all | solution.py:274
  66.9 81.0 %reduce-scatter.2.cloned.1.call-start = ((), (), s32[]{:S(2)}) async-start(), calls=%async_computation.6 | async-start | bytes 2228224 | tf_op jit(solution)/shard_map/reduce_scatter | solution.py:279
  66.9 1.5 copy-start
  128.1 7.2 %collective-permute-start.1 = (bf16[2048,256]{1,0:T(8,128)(2,1)S(1)}, bf16[2048,256]{1,0:T(8,128)(2,1)S(1)}, u32[]{:S(2)}, u32[]{:S(2)}) collective-permute-start(bf16[2048,256]{1,0:T(8,128)(2,1)S(1)} %bitcast.24), channel_id=1, source_target_pairs={{0,1},{1,0},{2,3},{3,2},{4,5},{5,4},{6,7},{7,6},{8,9},{9,8},{10,11... | collective-permute-start | bytes 3145736 | tf_op jit(solution)/shard_map/ppermute | solution.py:296
  138.1 27.7 %all-to-all-start.2 = ((bf16[8,128,256]{2,1,0:T(8,128)(2,1)}), bf16[8,128,256]{2,1,0:T(8,128)(2,1)S(1)}, u32[]{:S(2)}, u32[]{:S(2)}) async-start(bf16[8,128,256]{2,1,0:T(8,128)(2,1)} %shard_map.68), calls=%async_computation.2 | async-start | bytes 1048576 | tf_op jit(solution)/shard_map/all_to_all | solution.py:240
  148.8 17.1 %collective-permute-start.2 = (f32[64,256]{1,0:T(8,128)S(1)}, f32[64,256]{1,0:T(8,128)S(1)}, u32[]{:S(2)}, u32[]{:S(2)}) collective-permute-start(f32[64,256]{1,0:T(8,128)S(1)} %get-tuple-element.9), channel_id=1, source_target_pairs={{0,0},{1,32},{16,16},{17,48},{32,1},{33,33},{48,17},{49,49},{2,2},... | collective-permute-start | bytes 196616 | tf_op jit(solution)/shard_map/ppermute | solution.py:291
  154.2 11.7 %collective-permute-start.3 = (f32[64,256]{1,0:T(8,128)S(1)}, f32[64,256]{1,0:T(8,128)S(1)}, u32[]{:S(2)}, u32[]{:S(2)}) collective-permute-start(f32[64,256]{1,0:T(8,128)S(1)} %get-tuple-element.10), channel_id=1, source_target_pairs={{0,16},{1,48},{16,0},{17,32},{32,17},{33,49},{48,1},{49,33},{2,18}... | collective-permute-start | bytes 196616 | tf_op jit(solution)/shard_map/ppermute | solution.py:291
Sparse Core Ops, SparseCore 0:
  9.4 44.3 all-gather.1
  74.0 62.8 reduce-scatter.1

commit v4 on v3

--- a/solution.py
+++ b/solution.py
@@ -156,29 +156,23 @@
     )(rows, cols, *sent, weights)
 
 
-def pick_kernel(hot, *refs):
-    *parts, out = refs
-    at = 0
-    for part in parts:
-        depth = part.shape[1]
-        picked = jnp.dot(hot[...], part[...], preferred_element_type=jnp.float32)
-        out[:, at : at + depth] = picked.astype(out.dtype)
-        at += depth
-
-
-def pick_rows(hot, parts):
+def pick_kernel(hot, part, *refs):
+    refs[-1][...] = jnp.dot(hot[...], part[...], preferred_element_type=jnp.float32).astype(jnp.bfloat16)
+
+
+def pick_rows(hot, part, width, *earlier):
     picks, count = hot.shape
-    depth = sum(a.shape[1] for a in parts)
+    depth = part.shape[1]
     return pl.pallas_call(
         pick_kernel,
-        grid=(2,),
-        in_specs=[pl.BlockSpec((picks // 2, count), lambda g: (g, 0))]
-        + [pl.BlockSpec(a.shape, lambda g: (0, 0)) for a in parts],
-        out_specs=pl.BlockSpec((picks // 2, depth), lambda g: (g, 0)),
+        grid=(depth // width,),
+        in_specs=[pl.BlockSpec((picks, count), lambda g: (0, 0)), pl.BlockSpec((count, width), lambda g: (0, g))]
+        + [pl.BlockSpec(memory_space=pl.ANY)] * len(earlier),
+        out_specs=pl.BlockSpec((picks, width), lambda g: (0, g)),
         out_shape=jax.ShapeDtypeStruct((picks, depth), jnp.bfloat16),
         compiler_params=pltpu.CompilerParams(vmem_limit_bytes=56 * 2**20),
         cost_estimate=pl.CostEstimate(flops=10**9, bytes_accessed=4_000_000, transcendentals=0),
-    )(hot, *parts)
+    )(hot, part, *earlier)
 
 
 def base_kernel(tokens, weights, out):
@@ -270,7 +264,7 @@
         core_ref, own_blocks, other_blocks, lists[:, None], token[None, :], seq_count
     )
 
-    picked = pick_rows(hot, (gathered,))
+    picked = pick_rows(hot, gathered, 2 * LANES)
     sent = lax.all_to_all(picked.reshape(columns * 2, half, ff_local), CHIPS, split_axis=0, concat_axis=0, tiled=True)
     delta = delta_products(rows, cols, [sent], spread, seq_count, width)
     received = lax.all_to_all(delta, SEQ, split_axis=0, concat_axis=0, tiled=True)

time: 175 us -> 175 us (level)
  Pallas kernels: 34.2 us -> 36.6 us
  starting transfers between devices: 45.5 us -> 43.1 us
    all_to_all x1, starting transfers between devices: 9.78 us -> 7.36 us  [plane_sum(): parts = lax.all_to_all(values, 'z', split_axis=0, concat_axis=0, tiled=True)]
    pallas_call x1, Pallas kernels: 3.84 us -> 6.24 us  [pick_rows(): pl.pallas_call(pick_kernel, grid=(depth // width,), in_specs=[pl.BlockSpe...]
  transfers between devices with their start and end apart: 9 -> 9, of which waited for: 4 -> 4; matrix products, arithmetic and copies ran while one was open for 5% -> 5% of each run, Pallas kernels for 20% -> 21%
where the time goes in v4:
time: 175 us; the launch traced here: 173 us
  starting transfers between devices  43.1 us (25%)
  waiting for transfers between devices  38.4 us (22%)
  Pallas kernels  36.6 us (21%)
  blocking collectives  30.8 us (18%)
  between operations  13.6 us (8%)
  local copies, waits for them, and re-layouts  9.64 us (6%)
    all_to_all x1, blocking collectives, per_device(): lax.all_to_all(delta, SEQ, split_axis=0, concat_axis=0, tiled=True)  30.8 us
    all_to_all x1, waiting for transfers between devices, per_device(): lax.all_to_all(picked.reshape(columns * 2, half, ff_local), CHIPS, split_...  15.8 us
    pallas_call x1, Pallas kernels, spread_blocks(): pl.pallas_call(spread_kernel, grid_spec=pltpu.PrefetchScalarGridSpec(num_...  13.3 us
    all_gather x1, waiting for transfers between devices, per_device(): gathered = lax.all_gather(hidden, 'y', axis=0, tiled=True)  10.4 us
    all_to_all x1, starting transfers between devices, per_device(): lax.all_to_all(picked.reshape(columns * 2, half, ff_local), CHIPS, split_...  9.2 us
    all_to_all x1, waiting for transfers between devices, plane_sum(): parts = lax.all_to_all(values, 'z', split_axis=0, concat_axis=0, tiled=True)  9.01 us
    ppermute x1, starting transfers between devices, per_device(): other_blocks = lax.ppermute(own_blocks, 'core', CORE_SWAP)  8.78 us
    ppermute x2, starting transfers between devices, per_device(): blocks.append(lax.ppermute(mine, CHIPS, pairs))  8.02 us
  transfers between devices with their start and end apart: 9, of which 4 were waited for; matrix products, arithmetic and copies ran while one was open for 5% of the time, Pallas kernels for 21%

profile of v4, /device:TPU:1, one launch (start us, length us, event | category | flops | bytes accessed | tf_op | source)
XLA Modules:
  0.0 173.4 jit_solution(7111943488735645289)
XLA Ops:
  6.5 0.0 all-gather.2.cloned.1.call-start
  6.5 0.7 all-gather.2.cloned.1.call-update
  7.3 3.3 %broadcast_in_dim.5 = bf16[4,1792,256]{2,1,0:T(8,128)(2,1)} broadcast(bf16[1792,256]{1,0:T(8,128)(2,1)} %param.8), dimensions={1,2} | broadcast | bytes 4587520 | tf_op jit(solution)/shard_map/broadcast_in_dim | solution.py:251
  10.5 4.8 %all-to-all-start.3 = ((bf16[4,1792,256]{2,1,0:T(8,128)(2,1)}), bf16[4,1792,256]{2,1,0:T(8,128)(2,1)}, u32[]{:S(2)}, u32[]{:S(2)}) async-start(bf16[4,1792,256]{2,1,0:T(8,128)(2,1)} %broadcast_in_dim.5), calls=%async_computation.3 | async-start | bytes 7340032 | tf_op jit(solution)/shard_map/all_to_all | solution.py:252
  15.3 0.0 copy-start.2
  15.4 2.1 %copy.14 = bf16[32,8,32,128]{3,2,1,0:T(8,128)(2,1)S(1)} copy(bf16[32,8,32,128]{3,1,2,0:T(8,128)(2,1)} %bitcast.29) | data formatting | bytes 4194304
  17.4 0.0 copy-start.1
  17.4 8.8 %collective-permute-start = (bf16[256,32,128]{2,1,0:T(8,128)(2,1)S(1)}, bf16[256,32,128]{2,1,0:T(8,128)(2,1)}, u32[]{:S(2)}, u32[]{:S(2)}) collective-permute-start(bf16[256,32,128]{2,1,0:T(8,128)(2,1)S(1)} %bitcast.26), channel_id=1, source_target_pairs={{0,1},{1,0},{2,3},{3,2},{4,5},{5,4},{6,7},{7,6},{8,9},{9,8},{10,11... | collective-permute-start | bytes 6291464 | tf_op jit(solution)/shard_map/ppermute | solution.py:255
  26.2 0.0 copy-done.2
  26.3 0.9 copy.10.lists
  27.2 0.6 fusion.2.tokens
  27.8 2.4 %collective-permute-done.other = bf16[256,32,128]{2,1,0:T(8,128)(2,1)} collective-permute-done((bf16[256,32,128]{2,1,0:T(8,128)(2,1)S(1)}, bf16[256,32,128]{2,1,0:T(8,128)(2,1)}, u32[]{:S(2)}, u32[]{:S(2)}) %collective-permute-start) | collective-permute-done | bytes 2097184 | tf_op jit(solution)/shard_map/ppermute | solution.py:255
  30.1 0.0 copy-done.1
  30.1 13.3 %shard_map.64 = (bf16[2,256,64,128]{3,2,1,0:T(8,128)(2,1)}, bf16[512,512]{1,0:T(8,128)(2,1)}) custom-call(s32[1]{0:T(128)} %bitcast.core, bf16[256,32,128]{2,1,0:T(8,128)(2,1)} %bitcast.27, bf16[256,32,128]{2,1,0:T(8,128)(2,1)} %collective-permute-done.other, s32[512,1]{1,0:T(8,128)} %copy.10.lists, s32[1,512]{1,0:T(1,128)} %fusion.2.tokens), custom_call_target="tpu_custom_call" | custom-call | bytes 40000000 | tf_op jit(solution)/shard_map/pallas_call | solution.py:43
  43.4 10.4 %all-gather.2.cloned.1.call-done.part.tokens = bf16[512,1792]{1,0:T(8,128)(2,1)} async-done(((bf16[64,1792]{1,0:T(8,128)(2,1)}), bf16[512,1792]{1,0:T(8,128)(2,1)}) %all-gather.2.cloned.1.call-update) | async-done | bytes 1835024 | tf_op jit(solution)/shard_map/all_gather | solution.py:250
  53.9 6.2 %shard_map.65 = bf16[512,1792]{1,0:T(8,128)(2,1)} custom-call(bf16[512,512]{1,0:T(8,128)(2,1)} %get-tuple-element.7.hot, bf16[512,1792]{1,0:T(8,128)(2,1)} %all-gather.2.cloned.1.call-done.part.tokens), custom_call_target="tpu_custom_call" | custom-call | flops 1000000000 | bytes 4000000 | tf_op jit(solution)/shard_map/pallas_call | solution.py:166
  60.1 0.0 all-to-all-done.3.weights
  60.1 9.2 %all-to-all-start = ((bf16[8,64,1792]{2,1,0:T(8,128)(2,1)}), bf16[8,64,1792]{2,1,0:T(8,128)(2,1)S(1)}, u32[]{:S(2)}, u32[]{:S(2)}) async-start(bf16[8,64,1792]{2,1,0:T(8,128)(2,1)} %bitcast.28), calls=%async_computation | async-start | bytes 3670016 | tf_op jit(solution)/shard_map/all_to_all | solution.py:268
  69.3 0.0 reduce-scatter.2.cloned.1.call-start
  69.3 0.0 copy-start
  69.3 1.5 copy-done
  70.8 5.4 %shard_map.69 = f32[8,2,2,64,256]{4,3,2,1,0:T(8,128)} custom-call(bf16[512,1792]{1,0:T(8,128)(2,1)S(1)} %copy-done, bf16[4,1792,256]{2,1,0:T(8,128)(2,1)} %all-to-all-done.3.weights), custom_call_target="tpu_custom_call" | custom-call | flops 2000000000 | bytes 8000000 | tf_op jit(solution)/shard_map/pallas_call | solution.py:186
  76.2 0.0 reduce-scatter.2.cloned.1.call-update
  76.3 0.8 dynamic-slice_bitcast_fusion.3
  77.0 15.8 %all-to-all-done.refs_0_ = bf16[8,64,1792]{2,1,0:T(8,128)(2,1)S(1)} async-done(((bf16[8,64,1792]{2,1,0:T(8,128)(2,1)}), bf16[8,64,1792]{2,1,0:T(8,128)(2,1)S(1)}, u32[]{:S(2)}, u32[]{:S(2)}) %all-to-all-start) | async-done | bytes 1835040 | tf_op jit(solution)/shard_map/all_to_all | solution.py:268
  92.8 6.9 %shard_map.66 = bf16[32,64,256]{2,1,0:T(8,128)(2,1)S(1)} custom-call(s32[2,256]{1,0:T(2,128)S(1)} %get-tuple-element.14.rows, s32[2,256]{1,0:T(2,128)S(1)} %get-tuple-element.13.cols, bf16[8,64,1792]{2,1,0:T(8,128)(2,1)S(1)} %all-to-all-done.refs_0_, bf16[2,256,64,128]{3,2,1,0:T(8,128)(2,1)} %get-tuple-element.8.refs_1_), custom_call_target="tpu_custom_call" | custom-call | flops 2000000000 | bytes 20000000 | tf_op jit(solution)/shard_map/pallas_call | solution.py:139
  99.7 30.8 %all_to_all.20 = bf16[32,64,256]{2,1,0:T(8,128)(2,1)S(1)} all-to-all(bf16[32,64,256]{2,1,0:T(8,128)(2,1)S(1)} %shard_map.66), channel_id=1, replica_groups=mesh['y'=8,'x'=4,'z'=8,'core'=2] {'y','x'}, dimensions={0} | all-to-all | bytes 2097152 | tf_op jit(solution)/shard_map/all_to_all | solution.py:270
  130.5 4.9 %collective-permute-start.1 = (bf16[2048,256]{1,0:T(8,128)(2,1)S(1)}, bf16[2048,256]{1,0:T(8,128)(2,1)S(1)}, u32[]{:S(2)}, u32[]{:S(2)}) collective-permute-start(bf16[2048,256]{1,0:T(8,128)(2,1)S(1)} %bitcast.24), channel_id=1, source_target_pairs={{0,1},{1,0},{2,3},{3,2},{4,5},{5,4},{6,7},{7,6},{8,9},{9,8},{10,11... | collective-permute-start | bytes 3145736 | tf_op jit(solution)/shard_map/ppermute | solution.py:290
  135.4 0.1 reshape.95
  135.6 0.1 reshape.100.lists
  135.7 0.1 reshape.96.lists
  135.7 2.0 %shard_map.67.refs_0_ = bf16[8,128,256]{2,1,0:T(8,128)(2,1)S(1)} custom-call(s32[1]{0:T(128)} %bitcast.core, s32[1,2048]{1,0:T(1,128)S(1)} %reshape.100.lists, bf16[2048,256]{1,0:T(8,128)(2,1)S(1)} %bitcast.25), custom_call_target="tpu_custom_call" | custom-call | flops 1000000000 | bytes 4000000 | tf_op jit(solution)/shard_map/pallas_call | solution.py:215
  137.7 0.0 collective-permute-done.1.rows
  137.7 2.8 %shard_map.68 = bf16[8,128,256]{2,1,0:T(8,128)(2,1)} custom-call(s32[1]{0:T(128)} %bitcast.core, s32[1,2048]{1,0:T(1,128)S(1)} %reshape.96.lists, bf16[2048,256]{1,0:T(8,128)(2,1)S(1)} %collective-permute-done.1.rows, bf16[8,128,256]{2,1,0:T(8,128)(2,1)S(1)} %shard_map.67.refs_0_), custom_call_target="tpu_custom_call" | custom-call | flops 1000000000 | bytes 4000000 | tf_op jit(solution)/shard_map/pallas_call | solution.py:215
  140.5 7.4 %all-to-all-start.2 = ((bf16[8,128,256]{2,1,0:T(8,128)(2,1)}), bf16[8,128,256]{2,1,0:T(8,128)(2,1)S(1)}, u32[]{:S(2)}, u32[]{:S(2)}) async-start(bf16[8,128,256]{2,1,0:T(8,128)(2,1)} %shard_map.68), calls=%async_computation.2 | async-start | bytes 1048576 | tf_op jit(solution)/shard_map/all_to_all | solution.py:234
  147.9 0.0 reduce-scatter.2.cloned.1.call-done
  147.9 0.9 dynamic-slice_bitcast_fusion.1
  148.8 5.4 %collective-permute-start.2 = (f32[64,256]{1,0:T(8,128)S(1)}, f32[64,256]{1,0:T(8,128)S(1)}, u32[]{:S(2)}, u32[]{:S(2)}) collective-permute-start(f32[64,256]{1,0:T(8,128)S(1)} %get-tuple-element.9), channel_id=1, source_target_pairs={{0,0},{1,32},{16,16},{17,48},{32,1},{33,33},{48,17},{49,49},{2,2},... | collective-permute-start | bytes 196616 | tf_op jit(solution)/shard_map/ppermute | solution.py:285
  154.2 2.6 %collective-permute-start.3 = (f32[64,256]{1,0:T(8,128)S(1)}, f32[64,256]{1,0:T(8,128)S(1)}, u32[]{:S(2)}, u32[]{:S(2)}) collective-permute-start(f32[64,256]{1,0:T(8,128)S(1)} %get-tuple-element.10), channel_id=1, source_target_pairs={{0,16},{1,48},{16,0},{17,32},{32,17},{33,49},{48,1},{49,33},{2,18}... | collective-permute-start | bytes 196616 | tf_op jit(solution)/shard_map/ppermute | solution.py:285
  156.8 9.0 %all-to-all-done.2 = bf16[8,128,256]{2,1,0:T(8,128)(2,1)S(1)} async-done(((bf16[8,128,256]{2,1,0:T(8,128)(2,1)}), bf16[8,128,256]{2,1,0:T(8,128)(2,1)S(1)}, u32[]{:S(2)}, u32[]{:S(2)}) %all-to-all-start.2) | async-done | bytes 524320 | tf_op jit(solution)/shard_map/all_to_all | solution.py:234
  165.8 0.1 convert_reduce_fusion
  165.9 0.0 collective-permute-done.2
  165.9 0.0 collective-permute-done.3
  165.9 0.7 fusion.1
  (3 shorter events, 0.0 us)
Async XLA Ops:
  6.5 47.3 %all-gather.2.cloned.1.call-start = ((), (), s32[]{:S(2)}) async-start(), calls=%async_computation.5 | async-start | bytes 2064384 | tf_op jit(solution)/shard_map/all_gather | solution.py:250
  10.5 49.6 %all-to-all-start.3 = ((bf16[4,1792,256]{2,1,0:T(8,128)(2,1)}), bf16[4,1792,256]{2,1,0:T(8,128)(2,1)}, u32[]{:S(2)}, u32[]{:S(2)}) async-start(bf16[4,1792,256]{2,1,0:T(8,128)(2,1)} %broadcast_in_dim.5), calls=%async_computation.3 | async-start | bytes 7340032 | tf_op jit(solution)/shard_map/all_to_all | solution.py:252
  15.3 10.9 %copy-start.2 = (s32[32,128]{1,0:T(8,128)S(1)}, s32[32,128]{1,0:T(8,128)}, u32[]{:S(2)}) copy-start(s32[32,128]{1,0:T(8,128)} %param.12) | copy-start | bytes 49156
  17.4 12.7 %copy-start.1 = (bf16[32,8,32,128]{3,2,1,0:T(8,128)(2,1)}, bf16[32,8,32,128]{3,2,1,0:T(8,128)(2,1)S(1)}, u32[]{:S(2)}) copy-start(bf16[32,8,32,128]{3,2,1,0:T(8,128)(2,1)S(1)} %copy.14) | copy-start | bytes 6291460
  17.4 12.7 %collective-permute-start = (bf16[256,32,128]{2,1,0:T(8,128)(2,1)S(1)}, bf16[256,32,128]{2,1,0:T(8,128)(2,1)}, u32[]{:S(2)}, u32[]{:S(2)}) collective-permute-start(bf16[256,32,128]{2,1,0:T(8,128)(2,1)S(1)} %bitcast.26), channel_id=1, source_target_pairs={{0,1},{1,0},{2,3},{3,2},{4,5},{5,4},{6,7},{7,6},{8,9},{9,8},{10,11... | collective-permute-start | bytes 6291464 | tf_op jit(solution)/shard_map/ppermute | solution.py:255
  60.1 32.7 %all-to-all-start = ((bf16[8,64,1792]{2,1,0:T(8,128)(2,1)}), bf16[8,64,1792]{2,1,0:T(8,128)(2,1)S(1)}, u32[]{:S(2)}, u32[]{:S(2)}) async-start(bf16[8,64,1792]{2,1,0:T(8,128)(2,1)} %bitcast.28), calls=%async_computation | async-start | bytes 3670016 | tf_op jit(solution)/shard_map/all_to_all | solution.py:268
  69.3 78.6 %reduce-scatter.2.cloned.1.call-start = ((), (), s32[]{:S(2)}) async-start(), calls=%async_computation.6 | async-start | bytes 2228224 | tf_op jit(solution)/shard_map/reduce_scatter | solution.py:273
  69.3 1.5 copy-start
  130.5 7.2 %collective-permute-start.1 = (bf16[2048,256]{1,0:T(8,128)(2,1)S(1)}, bf16[2048,256]{1,0:T(8,128)(2,1)S(1)}, u32[]{:S(2)}, u32[]{:S(2)}) collective-permute-start(bf16[2048,256]{1,0:T(8,128)(2,1)S(1)} %bitcast.24), channel_id=1, source_target_pairs={{0,1},{1,0},{2,3},{3,2},{4,5},{5,4},{6,7},{7,6},{8,9},{9,8},{10,11... | collective-permute-start | bytes 3145736 | tf_op jit(solution)/shard_map/ppermute | solution.py:290
  140.5 25.3 %all-to-all-start.2 = ((bf16[8,128,256]{2,1,0:T(8,128)(2,1)}), bf16[8,128,256]{2,1,0:T(8,128)(2,1)S(1)}, u32[]{:S(2)}, u32[]{:S(2)}) async-start(bf16[8,128,256]{2,1,0:T(8,128)(2,1)} %shard_map.68), calls=%async_computation.2 | async-start | bytes 1048576 | tf_op jit(solution)/shard_map/all_to_all | solution.py:234
  148.8 17.1 %collective-permute-start.2 = (f32[64,256]{1,0:T(8,128)S(1)}, f32[64,256]{1,0:T(8,128)S(1)}, u32[]{:S(2)}, u32[]{:S(2)}) collective-permute-start(f32[64,256]{1,0:T(8,128)S(1)} %get-tuple-element.9), channel_id=1, source_target_pairs={{0,0},{1,32},{16,16},{17,48},{32,1},{33,33},{48,17},{49,49},{2,2},... | collective-permute-start | bytes 196616 | tf_op jit(solution)/shard_map/ppermute | solution.py:285
  154.2 11.7 %collective-permute-start.3 = (f32[64,256]{1,0:T(8,128)S(1)}, f32[64,256]{1,0:T(8,128)S(1)}, u32[]{:S(2)}, u32[]{:S(2)}) collective-permute-start(f32[64,256]{1,0:T(8,128)S(1)} %get-tuple-element.10), channel_id=1, source_target_pairs={{0,16},{1,48},{16,0},{17,32},{32,17},{33,49},{48,1},{49,33},{2,18}... | collective-permute-start | bytes 196616 | tf_op jit(solution)/shard_map/ppermute | solution.py:285
Sparse Core Ops, SparseCore 0:
  9.4 44.3 all-gather.1
  76.4 59.5 reduce-scatter.1

commit v5 on v4

--- a/solution.py
+++ b/solution.py
@@ -247,9 +247,10 @@
     slots = delta_blocks.shape[1]
     core_ref = core.reshape(1).astype(jnp.int32)
 
-    gathered = lax.all_gather(hidden, "y", axis=0, tiled=True)
-    copies = jnp.broadcast_to(down_weight[None], (columns, ff_local, width))
-    weights = lax.all_to_all(copies, "x", split_axis=0, concat_axis=0, tiled=True)
+    copies = jnp.broadcast_to(hidden[None], (lines, own_tokens, ff_local))
+    gathered = lax.all_to_all(copies, "y", split_axis=0, concat_axis=0, tiled=True)
+    gathered = gathered.reshape(lines * own_tokens, ff_local)
+    weights = lax.all_gather(down_weight, "x", axis=0, tiled=False)
 
     own_blocks = delta_blocks[0].reshape(slots, BLK // 2, 2 * BLK)
     other_blocks = lax.ppermute(own_blocks, "core", CORE_SWAP)

time: 175 us -> 184 us (1.051)
  waiting for transfers between devices: 38.4 us -> 47.2 us
  local copies, waits for them, and re-layouts: 9.64 us -> 13.2 us
    all_to_all x1, waiting for transfers between devices: 0.01 us -> 18 us  [per_device(): lax.all_to_all(copies, 'y', split_axis=0, concat_axis=0, tiled=True)]
    all_gather x1, waiting for transfers between devices: 10.4 us -> 0.01 us  [per_device(): weights = lax.all_gather(down_weight, 'x', axis=0, tiled=False)]
    unnamed x7 -> x11, local copies, waits for them, and re-layouts: 3.58 us -> 8.1 us
    ppermute x1, starting transfers between devices: 8.78 us -> 4.73 us  [per_device(): other_blocks = lax.ppermute(own_blocks, 'core', CORE_SWAP)]
    all_to_all x1, starting transfers between devices: 4.84 us -> 7.65 us  [per_device(): lax.all_to_all(copies, 'y', split_axis=0, concat_axis=0, tiled=True)]
    all_to_all x1, starting transfers between devices: 7.36 us -> 10 us  [plane_sum(): parts = lax.all_to_all(values, 'z', split_axis=0, concat_axis=0, tiled=True)]
    pallas_call x1, Pallas kernels: 5.41 us -> 2.81 us  [base_products(): pl.pallas_call(base_kernel, grid=(columns,), in_specs=[pl.BlockSpec((coun...]
    all_to_all x1, starting transfers between devices: 9.2 us -> 7.32 us  [per_device(): lax.all_to_all(picked.reshape(columns * 2, half, ff_local), CHIPS, split_...]
  transfers between devices with their start and end apart: 9 -> 9, of which waited for: 4 -> 4; matrix products, arithmetic and copies ran while one was open for 5% -> 5% of each run, Pallas kernels for 21% -> 19%
where the time goes in v5:
time: 184 us; the launch traced here: 183 us
  waiting for transfers between devices  47.2 us (26%)
  starting transfers between devices  42.5 us (23%)
  Pallas kernels  35.6 us (19%)
  blocking collectives  29.1 us (16%)
  between operations  13.6 us (7%)
  local copies, waits for them, and re-layouts  13.2 us (7%)
    all_to_all x1, blocking collectives, per_device(): lax.all_to_all(delta, SEQ, split_axis=0, concat_axis=0, tiled=True)  29.1 us
    all_to_all x1, waiting for transfers between devices, per_device(): lax.all_to_all(copies, 'y', split_axis=0, concat_axis=0, tiled=True)  18 us
    all_to_all x1, waiting for transfers between devices, per_device(): lax.all_to_all(picked.reshape(columns * 2, half, ff_local), CHIPS, split_...  16.6 us
    pallas_call x1, Pallas kernels, spread_blocks(): pl.pallas_call(spread_kernel, grid_spec=pltpu.PrefetchScalarGridSpec(num_...  13.4 us
    all_to_all x1, starting transfers between devices, plane_sum(): parts = lax.all_to_all(values, 'z', split_axis=0, concat_axis=0, tiled=True)  10 us
    all_to_all x1, waiting for transfers between devices, plane_sum(): parts = lax.all_to_all(values, 'z', split_axis=0, concat_axis=0, tiled=True)  9.36 us
    pallas_call x1, Pallas kernels, delta_products(): pl.pallas_call(delta_kernel, grid_spec=pltpu.PrefetchScalarGridSpec(num_s...  8.37 us
    unnamed x11, local copies, waits for them, and re-layouts  8.1 us
  transfers between devices with their start and end apart: 9, of which 4 were waited for; matrix products, arithmetic and copies ran while one was open for 5% of the time, Pallas kernels for 19%

profile of v5, /device:TPU:1, one launch (start us, length us, event | category | flops | bytes accessed | tf_op | source)
XLA Modules:
  0.0 182.6 jit_solution(15081761888725673516)
XLA Ops:
  6.5 0.0 all-gather.3.cloned.1.call-start
  6.5 0.7 all-gather.3.cloned.1.call-update
  7.3 2.3 %broadcast_in_dim.5 = bf16[8,64,1792]{2,1,0:T(8,128)(2,1)} broadcast(bf16[64,1792]{1,0:T(8,128)(2,1)} %param.7), dimensions={1,2} | broadcast | bytes 2064384 | tf_op jit(solution)/shard_map/broadcast_in_dim | solution.py:250
  9.6 7.7 %all-to-all-start = ((bf16[8,64,1792]{2,1,0:T(8,128)(2,1)}), bf16[8,64,1792]{2,1,0:T(8,128)(2,1)S(1)}, u32[]{:S(2)}, u32[]{:S(2)}) async-start(bf16[8,64,1792]{2,1,0:T(8,128)(2,1)} %broadcast_in_dim.5), calls=%async_computation | async-start | bytes 3670016 | tf_op jit(solution)/shard_map/all_to_all | solution.py:251
  17.2 0.0 copy-start.4
  17.2 3.5 %copy.14 = bf16[32,8,32,128]{3,2,1,0:T(8,128)(2,1)} copy(bf16[32,8,32,128]{3,1,2,0:T(8,128)(2,1)} %bitcast.33) | data formatting | bytes 4194304
  20.7 4.7 %collective-permute-start = (bf16[256,32,128]{2,1,0:T(8,128)(2,1)}, bf16[256,32,128]{2,1,0:T(8,128)(2,1)}, u32[]{:S(2)}, u32[]{:S(2)}) collective-permute-start(bf16[256,32,128]{2,1,0:T(8,128)(2,1)} %bitcast.17.own), channel_id=1, source_target_pairs={{0,1},{1,0},{2,3},{3,2},{4,5},{5,4},{6,7},{7,6},{8,9},{9,8},{10,11... | collective-permute-start | bytes 6291464 | tf_op jit(solution)/shard_map/ppermute | solution.py:256
  25.5 0.0 copy-done.4
  25.5 0.9 copy.10.lists
  26.4 0.6 fusion.2.tokens
  27.0 2.6 %collective-permute-done.other = bf16[256,32,128]{2,1,0:T(8,128)(2,1)} collective-permute-done((bf16[256,32,128]{2,1,0:T(8,128)(2,1)}, bf16[256,32,128]{2,1,0:T(8,128)(2,1)}, u32[]{:S(2)}, u32[]{:S(2)}) %collective-permute-start) | collective-permute-done | bytes 2097184 | tf_op jit(solution)/shard_map/ppermute | solution.py:256
  29.6 13.4 %shard_map.64 = (bf16[2,256,64,128]{3,2,1,0:T(8,128)(2,1)}, bf16[512,512]{1,0:T(8,128)(2,1)}) custom-call(s32[1]{0:T(128)} %bitcast.core, bf16[256,32,128]{2,1,0:T(8,128)(2,1)} %bitcast.17.own, bf16[256,32,128]{2,1,0:T(8,128)(2,1)} %collective-permute-done.other, s32[512,1]{1,0:T(8,128)} %copy.10.lists, s32[1,512]{1,0:T(1,128)} %fusion.2.tokens), custom_call_target="tpu_custom_call" | custom-call | bytes 40000000 | tf_op jit(solution)/shard_map/pallas_call | solution.py:43
  42.9 18.0 %all-to-all-done = bf16[8,64,1792]{2,1,0:T(8,128)(2,1)S(1)} async-done(((bf16[8,64,1792]{2,1,0:T(8,128)(2,1)}), bf16[8,64,1792]{2,1,0:T(8,128)(2,1)S(1)}, u32[]{:S(2)}, u32[]{:S(2)}) %all-to-all-start) | async-done | bytes 1835040 | tf_op jit(solution)/shard_map/all_to_all | solution.py:251
  60.9 0.0 copy-start
  60.9 1.2 copy-done
  62.1 6.3 %shard_map.65 = bf16[512,1792]{1,0:T(8,128)(2,1)} custom-call(bf16[512,512]{1,0:T(8,128)(2,1)} %get-tuple-element.7.hot, bf16[512,1792]{1,0:T(8,128)(2,1)} %bitcast.26), custom_call_target="tpu_custom_call" | custom-call | flops 1000000000 | bytes 4000000 | tf_op jit(solution)/shard_map/pallas_call | solution.py:166
  68.3 0.0 copy-start.1
  68.3 7.3 %all-to-all-start.1 = ((bf16[8,64,1792]{2,1,0:T(8,128)(2,1)}), bf16[8,64,1792]{2,1,0:T(8,128)(2,1)}, u32[]{:S(2)}, u32[]{:S(2)}) async-start(bf16[8,64,1792]{2,1,0:T(8,128)(2,1)} %bitcast.32), calls=%async_computation.1 | async-start | bytes 3670016 | tf_op jit(solution)/shard_map/all_to_all | solution.py:269
  75.7 0.0 reduce-scatter.2.cloned.1.call-start
  75.7 0.0 all-gather.3.cloned.1.call-done
  75.7 0.0 copy-done.1
  75.7 0.0 copy-start.3
  75.7 2.0 %copy-done.3 = bf16[7168,256]{1,0:T(8,128)(2,1)S(1)} copy-done((bf16[7168,256]{1,0:T(8,128)(2,1)S(1)}, bf16[7168,256]{1,0:T(8,128)(2,1)}, u32[]{:S(2)}) %copy-start.3) | copy-done | bytes 3670040
  77.7 2.8 %shard_map.69 = f32[8,2,2,64,256]{4,3,2,1,0:T(8,128)S(1)} custom-call(bf16[512,1792]{1,0:T(8,128)(2,1)S(1)} %bitcast.27, bf16[4,1792,256]{2,1,0:T(8,128)(2,1)S(1)} %bitcast.29), custom_call_target="tpu_custom_call" | custom-call | flops 2000000000 | bytes 8000000 | tf_op jit(solution)/shard_map/pallas_call | solution.py:186
  80.5 0.0 copy-start.2
  80.5 1.4 copy-done.2
  81.9 0.0 reduce-scatter.2.cloned.1.call-update
  82.0 0.8 dynamic-slice_bitcast_fusion.3
  82.7 16.6 %all-to-all-done.1.refs_0_ = bf16[8,64,1792]{2,1,0:T(8,128)(2,1)} async-done(((bf16[8,64,1792]{2,1,0:T(8,128)(2,1)}), bf16[8,64,1792]{2,1,0:T(8,128)(2,1)}, u32[]{:S(2)}, u32[]{:S(2)}) %all-to-all-start.1) | async-done | bytes 1835040 | tf_op jit(solution)/shard_map/all_to_all | solution.py:269
  99.3 8.4 %shard_map.66 = bf16[32,64,256]{2,1,0:T(8,128)(2,1)S(1)} custom-call(s32[2,256]{1,0:T(2,128)S(1)} %get-tuple-element.14.rows, s32[2,256]{1,0:T(2,128)S(1)} %get-tuple-element.13.cols, bf16[8,64,1792]{2,1,0:T(8,128)(2,1)} %all-to-all-done.1.refs_0_, bf16[2,256,64,128]{3,2,1,0:T(8,128)(2,1)} %get-tuple-element.8.refs_1_), custom_call_target="tpu_custom_call" | custom-call | flops 2000000000 | bytes 20000000 | tf_op jit(solution)/shard_map/pallas_call | solution.py:139
  107.7 29.1 %all_to_all.20 = bf16[32,64,256]{2,1,0:T(8,128)(2,1)S(1)} all-to-all(bf16[32,64,256]{2,1,0:T(8,128)(2,1)S(1)} %shard_map.66), channel_id=1, replica_groups=mesh['y'=8,'x'=4,'z'=8,'core'=2] {'y','x'}, dimensions={0} | all-to-all | bytes 2097152 | tf_op jit(solution)/shard_map/all_to_all | solution.py:271
  136.8 5.1 %collective-permute-start.1 = (bf16[2048,256]{1,0:T(8,128)(2,1)S(1)}, bf16[2048,256]{1,0:T(8,128)(2,1)S(1)}, u32[]{:S(2)}, u32[]{:S(2)}) collective-permute-start(bf16[2048,256]{1,0:T(8,128)(2,1)S(1)} %bitcast.30), channel_id=1, source_target_pairs={{0,1},{1,0},{2,3},{3,2},{4,5},{5,4},{6,7},{7,6},{8,9},{9,8},{10,11... | collective-permute-start | bytes 3145736 | tf_op jit(solution)/shard_map/ppermute | solution.py:291
  141.9 0.1 reshape.98
  142.1 0.1 reshape.104.lists
  142.1 0.1 reshape.99.lists
  142.2 2.0 %shard_map.67.refs_0_ = bf16[8,128,256]{2,1,0:T(8,128)(2,1)S(1)} custom-call(s32[1]{0:T(128)} %bitcast.core, s32[1,2048]{1,0:T(1,128)S(1)} %reshape.104.lists, bf16[2048,256]{1,0:T(8,128)(2,1)S(1)} %bitcast.31), custom_call_target="tpu_custom_call" | custom-call | flops 1000000000 | bytes 4000000 | tf_op jit(solution)/shard_map/pallas_call | solution.py:215
  144.2 0.0 collective-permute-done.1.rows
  144.2 2.8 %shard_map.68 = bf16[8,128,256]{2,1,0:T(8,128)(2,1)} custom-call(s32[1]{0:T(128)} %bitcast.core, s32[1,2048]{1,0:T(1,128)S(1)} %reshape.99.lists, bf16[2048,256]{1,0:T(8,128)(2,1)S(1)} %collective-permute-done.1.rows, bf16[8,128,256]{2,1,0:T(8,128)(2,1)S(1)} %shard_map.67.refs_0_), custom_call_target="tpu_custom_call" | custom-call | flops 1000000000 | bytes 4000000 | tf_op jit(solution)/shard_map/pallas_call | solution.py:215
  147.0 10.0 %all-to-all-start.3 = ((bf16[8,128,256]{2,1,0:T(8,128)(2,1)}), bf16[8,128,256]{2,1,0:T(8,128)(2,1)S(1)}, u32[]{:S(2)}, u32[]{:S(2)}) async-start(bf16[8,128,256]{2,1,0:T(8,128)(2,1)} %shard_map.68), calls=%async_computation.3 | async-start | bytes 1048576 | tf_op jit(solution)/shard_map/all_to_all | solution.py:234
  157.0 0.0 reduce-scatter.2.cloned.1.call-done
  157.1 0.9 dynamic-slice_bitcast_fusion.1
  157.9 5.1 %collective-permute-start.2 = (f32[64,256]{1,0:T(8,128)S(1)}, f32[64,256]{1,0:T(8,128)S(1)}, u32[]{:S(2)}, u32[]{:S(2)}) collective-permute-start(f32[64,256]{1,0:T(8,128)S(1)} %get-tuple-element.9), channel_id=1, source_target_pairs={{0,0},{1,32},{16,16},{17,48},{32,1},{33,33},{48,17},{49,49},{2,2},... | collective-permute-start | bytes 196616 | tf_op jit(solution)/shard_map/ppermute | solution.py:286
  163.0 2.6 %collective-permute-start.3 = (f32[64,256]{1,0:T(8,128)S(1)}, f32[64,256]{1,0:T(8,128)S(1)}, u32[]{:S(2)}, u32[]{:S(2)}) collective-permute-start(f32[64,256]{1,0:T(8,128)S(1)} %get-tuple-element.10), channel_id=1, source_target_pairs={{0,16},{1,48},{16,0},{17,32},{32,17},{33,49},{48,1},{49,33},{2,18}... | collective-permute-start | bytes 196616 | tf_op jit(solution)/shard_map/ppermute | solution.py:286
  165.6 9.4 %all-to-all-done.3 = bf16[8,128,256]{2,1,0:T(8,128)(2,1)S(1)} async-done(((bf16[8,128,256]{2,1,0:T(8,128)(2,1)}), bf16[8,128,256]{2,1,0:T(8,128)(2,1)S(1)}, u32[]{:S(2)}, u32[]{:S(2)}) %all-to-all-start.3) | async-done | bytes 524320 | tf_op jit(solution)/shard_map/all_to_all | solution.py:234
  175.0 0.1 convert_reduce_fusion
  175.1 0.0 collective-permute-done.2
  175.1 0.0 collective-permute-done.3
  175.1 0.7 fusion.1
  (3 shorter events, 0.1 us)
Async XLA Ops:
  6.5 69.1 %all-gather.3.cloned.1.call-start = ((), (), s32[]{:S(2)}) async-start(), calls=%async_computation.6 | async-start | bytes 4587520 | tf_op jit(solution)/shard_map/all_gather | solution.py:253
  9.6 51.3 %all-to-all-start = ((bf16[8,64,1792]{2,1,0:T(8,128)(2,1)}), bf16[8,64,1792]{2,1,0:T(8,128)(2,1)S(1)}, u32[]{:S(2)}, u32[]{:S(2)}) async-start(bf16[8,64,1792]{2,1,0:T(8,128)(2,1)} %broadcast_in_dim.5), calls=%async_computation | async-start | bytes 3670016 | tf_op jit(solution)/shard_map/all_to_all | solution.py:251
  17.2 8.2 %copy-start.4 = (s32[32,128]{1,0:T(8,128)S(1)}, s32[32,128]{1,0:T(8,128)}, u32[]{:S(2)}) copy-start(s32[32,128]{1,0:T(8,128)} %param.12) | copy-start | bytes 49156
  20.7 8.8 %collective-permute-start = (bf16[256,32,128]{2,1,0:T(8,128)(2,1)}, bf16[256,32,128]{2,1,0:T(8,128)(2,1)}, u32[]{:S(2)}, u32[]{:S(2)}) collective-permute-start(bf16[256,32,128]{2,1,0:T(8,128)(2,1)} %bitcast.17.own), channel_id=1, source_target_pairs={{0,1},{1,0},{2,3},{3,2},{4,5},{5,4},{6,7},{7,6},{8,9},{9,8},{10,11... | collective-permute-start | bytes 6291464 | tf_op jit(solution)/shard_map/ppermute | solution.py:256
  60.9 1.2 copy-start
  68.3 7.3 %copy-start.1 = (bf16[8,64,1792]{2,1,0:T(8,128)(2,1)S(1)}, bf16[8,64,1792]{2,1,0:T(8,128)(2,1)}, u32[]{:S(2)}) copy-start(bf16[8,64,1792]{2,1,0:T(8,128)(2,1)} %copy-done) | copy-start | bytes 5505028
  68.3 31.0 %all-to-all-start.1 = ((bf16[8,64,1792]{2,1,0:T(8,128)(2,1)}), bf16[8,64,1792]{2,1,0:T(8,128)(2,1)}, u32[]{:S(2)}, u32[]{:S(2)}) async-start(bf16[8,64,1792]{2,1,0:T(8,128)(2,1)} %bitcast.32), calls=%async_computation.1 | async-start | bytes 3670016 | tf_op jit(solution)/shard_map/all_to_all | solution.py:269
  75.7 81.4 %reduce-scatter.2.cloned.1.call-start = ((), (), s32[]{:S(2)}) async-start(), calls=%async_computation.5 | async-start | bytes 2228224 | tf_op jit(solution)/shard_map/reduce_scatter | solution.py:274
  75.7 2.0 %copy-start.3 = (bf16[7168,256]{1,0:T(8,128)(2,1)S(1)}, bf16[7168,256]{1,0:T(8,128)(2,1)}, u32[]{:S(2)}) copy-start(bf16[7168,256]{1,0:T(8,128)(2,1)} %all-gather.3.cloned.1.call-done) | copy-start | bytes 11010052
  80.5 1.4 copy-start.2
  136.8 7.4 %collective-permute-start.1 = (bf16[2048,256]{1,0:T(8,128)(2,1)S(1)}, bf16[2048,256]{1,0:T(8,128)(2,1)S(1)}, u32[]{:S(2)}, u32[]{:S(2)}) collective-permute-start(bf16[2048,256]{1,0:T(8,128)(2,1)S(1)} %bitcast.30), channel_id=1, source_target_pairs={{0,1},{1,0},{2,3},{3,2},{4,5},{5,4},{6,7},{7,6},{8,9},{9,8},{10,11... | collective-permute-start | bytes 3145736 | tf_op jit(solution)/shard_map/ppermute | solution.py:291
  147.0 28.0 %all-to-all-start.3 = ((bf16[8,128,256]{2,1,0:T(8,128)(2,1)}), bf16[8,128,256]{2,1,0:T(8,128)(2,1)S(1)}, u32[]{:S(2)}, u32[]{:S(2)}) async-start(bf16[8,128,256]{2,1,0:T(8,128)(2,1)} %shard_map.68), calls=%async_computation.3 | async-start | bytes 1048576 | tf_op jit(solution)/shard_map/all_to_all | solution.py:234
  157.9 17.1 %collective-permute-start.2 = (f32[64,256]{1,0:T(8,128)S(1)}, f32[64,256]{1,0:T(8,128)S(1)}, u32[]{:S(2)}, u32[]{:S(2)}) collective-permute-start(f32[64,256]{1,0:T(8,128)S(1)} %get-tuple-element.9), channel_id=1, source_target_pairs={{0,0},{1,32},{16,16},{17,48},{32,1},{33,33},{48,17},{49,49},{2,2},... | collective-permute-start | bytes 196616 | tf_op jit(solution)/shard_map/ppermute | solution.py:286
  163.0 12.0 %collective-permute-start.3 = (f32[64,256]{1,0:T(8,128)S(1)}, f32[64,256]{1,0:T(8,128)S(1)}, u32[]{:S(2)}, u32[]{:S(2)}) collective-permute-start(f32[64,256]{1,0:T(8,128)S(1)} %get-tuple-element.10), channel_id=1, source_target_pairs={{0,16},{1,48},{16,0},{17,32},{32,17},{33,49},{48,1},{49,33},{2,18}... | collective-permute-start | bytes 196616 | tf_op jit(solution)/shard_map/ppermute | solution.py:286
Sparse Core Ops, SparseCore 0:
  9.5 54.7 all-gather.2
  82.1 60.1 reduce-scatter.1
